TPU v7x, 32 devices: a whole 2x2x4 slice. The times are simulated.
32 devices in a mesh: dp: 8 (over y, x, core), tensor: 4 (over z).
Axes of the slice: x: 2, y: 2, z: 4, core: 2. Of those that a mesh axis runs over, the one named last changes fastest.
Arguments:
- tokens: bfloat16 [2048, 2560], P('dp'), may hold values from -6 to 6
- segments: int32 [2048], P('dp'), may hold values from 0 to 2047, as said below
- first_gain: float32 [2560], replicated, may hold values from 0.5 to 1.5
- x_weight: bfloat16 [2560, 10, 256], P('dp', None, 'tensor'), may hold values from -0.125 to 0.125
- y_weight: bfloat16 [2560, 10, 256], P('dp', None, 'tensor'), may hold values from -0.125 to 0.125
- conv_weight: float32 [4, 10, 256], P(None, None, 'tensor'), may hold values from -3 to 3
- conv_bias: float32 [10, 256], P(None, 'tensor'), may hold values from -3 to 3
- rate_weight: bfloat16 [10, 256, 256], P(None, None, 'tensor'), may hold values from -0.375 to 0.375
- input_weight: bfloat16 [10, 256, 256], P(None, None, 'tensor'), may hold values from -0.375 to 0.375
- rate_bias: float32 [10, 256], P(None, 'tensor'), may hold values from -4 to 4
- input_bias: float32 [10, 256], P(None, 'tensor'), may hold values from -4 to 4
- decay_logit: float32 [10, 256], P(None, 'tensor'), may hold values from 0.5 to 7
- out_weight: bfloat16 [10, 256, 2560], P(None, 'tensor', 'dp'), may hold values from -0.3125 to 0.3125
- second_gain: float32 [2560], replicated, may hold values from 0.5 to 1.5
- gate_weight: bfloat16 [2560, 7680], P('dp', 'tensor'), may hold values from -0.125 to 0.125
- up_weight: bfloat16 [2560, 7680], P('dp', 'tensor'), may hold values from -0.125 to 0.125
- down_weight: bfloat16 [7680, 2560], P('tensor', 'dp'), may hold values from -0.125 to 0.125
- cotangent: bfloat16 [2048, 2560], P('dp'), may hold values from -6 to 6
Outputs:
- block_out: bfloat16 [2048, 2560], P('dp')
- tokens_grad: float32 [2048, 2560], P('dp')
- first_gain_grad: float32 [2560], replicated
- x_weight_grad: float32 [2560, 10, 256], P('dp', None, 'tensor')
- y_weight_grad: float32 [2560, 10, 256], P('dp', None, 'tensor')
- conv_weight_grad: float32 [4, 10, 256], P(None, None, 'tensor')
- conv_bias_grad: float32 [10, 256], P(None, 'tensor')
- rate_weight_grad: float32 [10, 256, 256], P(None, None, 'tensor')
- input_weight_grad: float32 [10, 256, 256], P(None, None, 'tensor')
- rate_bias_grad: float32 [10, 256], P(None, 'tensor')
- input_bias_grad: float32 [10, 256], P(None, 'tensor')
- decay_logit_grad: float32 [10, 256], P(None, 'tensor')
- out_weight_grad: float32 [10, 256, 2560], P(None, 'tensor', 'dp')
- second_gain_grad: float32 [2560], replicated
- gate_weight_grad: float32 [2560, 7680], P('dp', 'tensor')
- up_weight_grad: float32 [2560, 7680], P('dp', 'tensor')
- down_weight_grad: float32 [7680, 2560], P('tensor', 'dp')
Inputs may be any that keep to these rules, and one draw needn't show every extreme that they name: `segments`: each aligned block of 256 tokens holds whole sequences: a token's value is the index of the first token of its sequence, values never fall, a sequence begins at the first token of every block, the last token of all forms a sequence of its own, and in some block other than the last one sequence fills all 256 tokens.
All inputs are finite; a program needn't handle non-finite values.
Results may differ from a plain program's by a relative error of at most 0.01.
Values may be sent and summed in bfloat16 or wider, within the bound.
No kernel may reach another device: no remote copies, remote signals or barrier semaphores. Data moves between devices by JAX's collectives and lax.ppermute only.
A program may use at most 256 MiB of HBM per device.

v0:
```python
from functools import partial

import jax
import jax.numpy as jnp
from jax import lax
from jax.experimental import pallas as pl
from jax.experimental.pallas import tpu as pltpu
from jax.sharding import PartitionSpec as P

eps = 1e-06
f32 = jnp.float32
bf16 = jnp.bfloat16
vmem = pl.BlockSpec(memory_space=pltpu.VMEM)
smem = pl.BlockSpec(memory_space=pltpu.SMEM)
MIB = 1024 * 1024
chunk_count = 3


def nn(a, b):
    return lax.dot_general(a, b, (((1,), (0,)), ((), ())), preferred_element_type=f32)


def nt(a, b):
    return lax.dot_general(a, b, (((1,), (1,)), ((), ())), preferred_element_type=f32)


def tn(a, b):
    return lax.dot_general(a, b, (((0,), (0,)), ((), ())), preferred_element_type=f32)


def full(v):
    zeros = (0,) * len(v.shape)
    return pl.BlockSpec(v.shape, lambda i: zeros, pipeline_mode=pl.Buffered(1))


def block(shape, *index):
    return pl.BlockSpec(shape, lambda i: index)


def hint_of(micros):
    return pl.CostEstimate(
        flops=1, bytes_accessed=max(1, int(micros * 3.0e6)), transcendentals=0
    )


hint = hint_of(0)


def call(kernel, outs, *args, scalars=0, mem=60, specs=None, out_specs=None, alias=None, scratch=(), micros=0, name=None):
    specs = specs or {}
    return pl.pallas_call(
        kernel,
        grid=(1,),
        out_shape=outs,
        in_specs=[smem] * scalars
        + [specs.get(i) or full(a) for i, a in enumerate(args) if i >= scalars],
        out_specs=out_specs or [full(s) for s in outs],
        scratch_shapes=scratch,
        input_output_aliases=alias or {},
        compiler_params=pltpu.CompilerParams(vmem_limit_bytes=mem * MIB),
        cost_estimate=hint_of(micros),
        name=name,
    )(*args)


def like(shape, dtype):
    return jax.ShapeDtypeStruct(shape, dtype)


def gelu_pair(v):
    c = 0.7978845608028654
    sq = v * v
    t = jnp.tanh(c * v * (1.0 + 0.044715 * sq))
    half = 0.5 * (1.0 + t)
    slope = half + 0.5 * v * (1.0 - t * t) * c * (1.0 + 3.0 * 0.044715 * sq)
    return v * half, slope


def one_less_exp(x):
    series = x * (
        1.0
        - x * (1 / 2) * (1.0 - x * (1 / 3) * (1.0 - x * (1 / 4) * (1.0 - x * (1 / 5) * (
            1.0 - x * (1 / 6) * (1.0 - x * (1 / 7) * (1.0 - x * (1 / 8)))))))
    )
    return jnp.where(x < 0.5, series, 1.0 - jnp.exp(-x))


def softplus(v):
    return jnp.maximum(v, 0.0) + jnp.log1p(jnp.exp(-jnp.abs(v)))


def sigmoid(v):
    return 1.0 / (1.0 + jnp.exp(-v))


def row_ids(shape):
    return lax.broadcasted_iota(jnp.int32, shape, 0)


def down_rows(v, steps, fill=0.0):
    return jnp.where(row_ids(v.shape) >= steps, pltpu.roll(v, steps, 0), fill)


def up_rows(v, steps, fill=0.0):
    rows = v.shape[0]
    return jnp.where(row_ids(v.shape) < rows - steps, pltpu.roll(v, rows - steps, 0), fill)


def scan_rows(decay, drive, shift):
    steps = 1
    while steps < decay.shape[0]:
        drive = decay * shift(drive, steps) + drive
        if steps * 2 < decay.shape[0]:
            decay = decay * shift(decay, steps, 1.0)
        steps *= 2
    return drive


def norm_first_kernel(size, z_ref, x_ref, one_ref, two_ref, rel_ref, out_ref, one_out, two_out):
    me = z_ref[1]
    gain = to_rel(me, size, one_ref[...].reshape(1, -1))
    rel = to_rel(me, size, x_ref[...].astype(f32))
    rel_ref[...] = rel.astype(bf16)
    inv = lax.rsqrt(jnp.mean(rel * rel, axis=1, keepdims=True) + eps)
    out_ref[...] = (rel * inv * gain).astype(bf16)
    one_out[...] = gain
    two_out[...] = to_rel(me, size, two_ref[...].reshape(1, -1))


def to_rel_kernel(size, z_ref, x_ref, rel_ref):
    rel_ref[...] = to_rel(z_ref[1], size, x_ref[...].astype(f32)).astype(bf16)


def shard_kernel(gate_ref, up_ref, down_ref, out_ref):
    width = gate_ref.shape[1]
    out_ref[:, :width] = gate_ref[...]
    out_ref[:, width : 2 * width] = up_ref[...]
    out_ref[:, 2 * width :] = down_ref[...]


def blocks_kernel(z_ref, rate_ref, input_ref, out_ref):
    units = rate_ref.shape[1]
    zero = jnp.zeros((units, units), bf16)
    for p in range(out_ref.shape[0]):
        for a in range(2):
            parts = [ref[2 * p + a].T for ref in (rate_ref, input_ref)]
            rows = []
            for k in range(4):
                row = []
                for part in parts:
                    one = jnp.zeros_like(zero)
                    for owner in range(4):
                        one = jnp.where(
                            (z_ref[0] ^ k) == owner, part[owner * units : (owner + 1) * units], one
                        )
                    row += [zero, one] if a else [one, zero]
                at = slice((2 * k + a) * units, (2 * k + a + 1) * units)
                out_ref[p, at, :] = jnp.concatenate(row, axis=1)


def land(pieces, w_ref, sems, first=0):
    copies, at = [], 0
    for n, piece in enumerate(pieces):
        rows = piece.shape[0]
        copy = pltpu.make_async_copy(piece, w_ref.at[pl.ds(at, rows)], sems.at[first + n])
        copy.start()
        copies.append((at, copy))
        at += rows
    return copies


def await_rows(copies, until):
    while copies and copies[0][0] < until:
        copies.pop(0)[1].wait()


def join_kernel(count, *refs):
    pieces, (first, second, sems) = refs[:-3], refs[-3:]
    copies = land(pieces[:count], first, sems) + land(pieces[count:], second, sems, count)
    for _, copy in copies:
        copy.wait()


def branch_kernel(nf_ref, taps_ref, bias_ref, mask_ref, *refs):
    pieces, (x_ref, conv_ref, w_ref, sems) = refs[:-4], refs[-4:]
    step = w_ref.shape[0] // 4
    copies = land(pieces, w_ref, sems)
    for i in range(4):
        rows = slice(i * step, (i + 1) * step)
        await_rows(copies, (i + 1) * step)
        part = nn(nf_ref[:, rows], w_ref[rows, :])
        x_ref[...] = part if i == 0 else x_ref[...] + part
    for c in range(0, x_ref.shape[1], 128):
        cols = slice(c, c + 128)
        x = x_ref[:, cols]
        total = x * taps_ref[0:1, cols] + bias_ref[:, cols]
        for lag in range(1, taps_ref.shape[0]):
            total = total + down_rows(x, lag) * mask_ref[lag - 1] * taps_ref[lag : lag + 1, cols]
        conv_ref[:, cols] = total.astype(bf16)


def mix_kernel(z_ref, nf_ref, hidden_ref, *refs):
    pieces = refs[:-9]
    y_ref, mixed_ref, o0, o1, o2, o3, total_ref, w_ref, sems = refs[-9:]
    width, half = y_ref.shape[1], len(pieces)
    step = w_ref.shape[1] // 4
    gate = land([p.at[:, pl.ds(0, width)] for p in pieces], w_ref.at[0], sems)
    out = land([p.at[:, pl.ds(width, width)] for p in pieces], w_ref.at[1], sems, half)
    for i in range(4):
        rows = slice(i * step, (i + 1) * step)
        await_rows(gate, (i + 1) * step)
        part = nn(nf_ref[:, rows], w_ref[0, rows, :])
        y_ref[...] = part if i == 0 else y_ref[...] + part
    for c in range(0, width, 128):
        cols = slice(c, c + 128)
        mixed_ref[:, cols] = (hidden_ref[:, cols] * gelu_pair(y_ref[:, cols])[0]).astype(bf16)
    for i in range(4):
        rows = slice(i * step, (i + 1) * step)
        await_rows(out, (i + 1) * step)
        total_ref[:, rows] = nt(mixed_ref[...], w_ref[1, rows, :])
    split_rows(z_ref, total_ref, (o0, o1, o2, o3))


def gates_of(rate, decay_logit, start):
    soft = softplus(-decay_logit)
    minus_log = 8.0 * rate * soft
    lost = one_less_exp(2.0 * minus_log)
    mult = jnp.where(start, 1.0, jnp.sqrt(lost))
    carried = jnp.where(start, 0.0, jnp.exp(-minus_log))
    return soft, mult, carried


def forward_scan_kernel(
    c0, c1, c2, c3, block_ref, rb_ref, ib_ref, dl_ref, mask_ref, rate_ref, entry_ref, hidden_ref
):
    start = mask_ref[0] == 0.0
    pre = nn(jnp.concatenate([c0[...], c1[...], c2[...], c3[...]], axis=1), block_ref[0])
    rate = sigmoid(pre[:, :128] + rb_ref[...])
    entry = sigmoid(pre[:, 128:] + ib_ref[...])
    _, mult, carried = gates_of(rate, dl_ref[...], start)
    driven = c0[...].astype(f32) * entry * mult
    rate_ref[...] = rate
    entry_ref[...] = entry
    hidden_ref[...] = scan_rows(carried, driven, down_rows)


def fetch(step, pieces, w_ref, sems):
    copies = []
    for side, group in enumerate(pieces):
        at = 0
        for piece in group:
            rows = piece.shape[0]
            cols = pl.ds(side * piece.shape[1], piece.shape[1])
            copies.append(
                pltpu.make_async_copy(piece, w_ref.at[pl.ds(at, rows), cols], sems.at[len(copies)])
            )
            at += rows

    @pl.when(step == 0)
    def _():
        for copy in copies:
            copy.start()

    return copies


def product(landing, left_ref, w_ref, total_ref):
    for copy in landing:
        copy.wait()
    rows = w_ref.shape[0] // 4
    for i in range(4):
        at = slice(i * rows, (i + 1) * rows)
        total_ref[:, at] = nt(left_ref[...], w_ref[at, :])


def backward_scan_kernel(count, z_ref, p0, p1, p2, p3, *refs):
    weights, refs = refs[:count], refs[count:]
    c0, c1, c2, c3, block_ref, dl_ref, y_ref, mask_ref, rate_ref, entry_ref, hidden_ref = refs[:11]
    g_ref, gy_ref, direct_ref, h1_ref, h2_ref, h3_ref, mine_ref, theirs_ref, sums_ref = refs[11:]

    @pl.when(pl.program_id(0) == 0)
    def _():
        assemble_kernel(z_ref, p0, p1, p2, p3, g_ref)

    start = mask_ref[0] == 0.0
    grad_mixed = nn(g_ref[...], jnp.concatenate([w[...] for w in weights], axis=0))
    hidden, rate, entry = hidden_ref[...], rate_ref[...], entry_ref[...]
    conv = c0[...].astype(f32)
    gelu_y, slope_y = gelu_pair(y_ref[...])
    gy_ref[...] = (grad_mixed * hidden * slope_y).astype(bf16)
    decay_logit = dl_ref[...]
    soft, mult, carried = gates_of(rate, decay_logit, start)
    state = scan_rows(up_rows(carried, 1), grad_mixed * gelu_y, up_rows)
    kept = carried * carried
    grad_log = jnp.where(
        start, 0.0, state * (down_rows(hidden, 1) * carried - conv * entry * kept / mult)
    )
    rate_low = (grad_log * (-8.0 * soft) * rate * (1.0 - rate)).astype(bf16)
    entry_low = (state * conv * mult * entry * (1.0 - entry)).astype(bf16)
    both = jnp.concatenate([rate_low, entry_low], axis=1)
    sums_ref[...] = jnp.concatenate(
        [
            jnp.sum(grad_log * rate, axis=0, keepdims=True) * (8.0 * sigmoid(-decay_logit)),
            jnp.sum(rate_low.astype(f32), axis=0, keepdims=True),
            jnp.sum(entry_low.astype(f32), axis=0, keepdims=True),
            jnp.zeros((5, 128), f32),
        ],
        axis=0,
    )
    heads = nt(both, block_ref[0])
    direct_ref[...] = state * entry * mult + heads[:, :128]
    h1_ref[...] = heads[:, 128:256].astype(bf16)
    h2_ref[...] = heads[:, 256:384]
    h3_ref[...] = heads[:, 384:].astype(bf16)
    units = jnp.concatenate([c0[...], c1[...], c2[...], c3[...]], axis=1)
    grads = tn(units, both)
    first = jnp.concatenate([grads[:, 0:64], grads[:, 128:192]], axis=1)
    second = jnp.concatenate([grads[:, 64:128], grads[:, 192:256]], axis=1)
    for k in range(4):
        even, odd = first[k * 128 : k * 128 + 64], second[k * 128 + 64 : k * 128 + 128]
        own = z_ref[1] % 2 == 0
        mine_ref[0, k] = jnp.where(own, even, odd).astype(bf16)
        theirs_ref[0, k] = jnp.where(own, odd, even).astype(bf16)


def conv_back_kernel(
    size, count, z_ref, direct_ref, r1, r2, x_ref, taps_ref, mask_ref, gy_ref, rel_ref, *refs
):
    weights, refs = refs[: 2 * count], refs[2 * count :]
    gx_ref, sums_ref, gain_ref, o0, o1, o2, o3, total_ref, w_ref, left_ref, sems = refs
    step, width = pl.program_id(0), left_ref.shape[1] // 2
    sides = (weights[:count], [w.at[:, pl.ds(0, width)] for w in weights[count:]])
    landing = fetch(step, sides, w_ref, sems)
    chan = left_ref.shape[1] // 2
    total = direct_ref[...] + r1[...].astype(f32) + r2[...].astype(f32)
    x = x_ref[...]
    grad = total * taps_ref[0:1]
    sums = [jnp.sum(total * x, axis=0, keepdims=True)]
    for lag in range(1, taps_ref.shape[0]):
        kept = total * mask_ref[lag - 1]
        grad = grad + up_rows(kept, lag) * taps_ref[lag : lag + 1]
        sums.append(jnp.sum(kept * down_rows(x, lag), axis=0, keepdims=True))
    low = grad.astype(bf16)
    gx_ref[...] = low
    sums.append(jnp.sum(total, axis=0, keepdims=True))
    sums.append(jnp.zeros((8 - len(sums), x.shape[1]), f32))
    sums_ref[...] = jnp.concatenate(sums, axis=0)
    left_ref[:, pl.ds(pl.multiple_of(step * 128, 128), 128)] = low
    left_ref[:, pl.ds(pl.multiple_of(chan + step * 128, 128), 128)] = gy_ref[...]

    @pl.when(step == pl.num_programs(0) - 1)
    def _():
        product(landing, left_ref, w_ref, total_ref)
        split_rows(z_ref, total_ref, (o0, o1, o2, o3))
        rel = rel_ref[...].astype(f32)
        inv = lax.rsqrt(jnp.mean(rel * rel, axis=1, keepdims=True) + eps)
        gain = jnp.sum(total_ref[...] * (rel * inv), axis=0, keepdims=True)
        gain_ref[...] = to_abs(z_ref[1], size, gain)


def split_rows(z_ref, total_ref, outs):
    rows = outs[0].shape[0]
    for k, out in enumerate(outs):
        at = pl.multiple_of((z_ref[0] ^ k) * rows, rows)
        out[...] = total_ref[pl.ds(at, rows), :].astype(out.dtype)


def assemble_kernel(z_ref, *refs):
    pieces, out_ref = refs[:-1], refs[-1]
    rows = pieces[0].shape[0]
    for k, piece in enumerate(pieces):
        at = pl.multiple_of((z_ref[0] ^ k) * rows, rows)
        out_ref[pl.ds(at, rows), :] = piece[...].astype(out_ref.dtype)


def to_abs(me, size, v):
    part = v.shape[1] // size

    def picked(v, places):
        return jnp.concatenate([v[:, p * part : (p + 1) * part] for p in places], axis=1)

    v = picked(v, [(s % 2) * (size // 2) + s // 2 for s in range(size)])
    bit = 1
    while bit < size:
        v = jnp.where((me // bit) % 2 == 1, picked(v, [s ^ bit for s in range(size)]), v)
        bit *= 2
    return v


def to_rel(me, size, v):
    part = v.shape[1] // size

    def picked(v, places):
        return jnp.concatenate([v[:, p * part : (p + 1) * part] for p in places], axis=1)

    bit = 1
    while bit < size:
        v = jnp.where((me // bit) % 2 == 1, picked(v, [s ^ bit for s in range(size)]), v)
        bit *= 2
    return picked(v, [2 * j + c for c in range(2) for j in range(size // 2)])


def sum_pieces(pieces):
    total = pieces[0][...]
    for piece in pieces[1:]:
        total = total + piece[...].astype(f32)
    return total


def my_rows(z_ref, ref, rows):
    return ref[pl.ds(pl.multiple_of(z_ref[0] * rows, rows), rows), :].astype(f32)


def norm_second_kernel(z_ref, x_ref, gain_ref, o0, o1, o2, res_ref, low_ref):
    residual = my_rows(z_ref, x_ref, res_ref.shape[0]) + sum_pieces((o0, o1, o2))
    inv = lax.rsqrt(jnp.mean(residual * residual, axis=1, keepdims=True) + eps)
    res_ref[...] = residual
    low_ref[...] = (residual * inv * gain_ref[...]).astype(bf16)


def norm_back(x, gain, grad):
    inv = lax.rsqrt(jnp.mean(x * x, axis=1, keepdims=True) + eps)
    unit = x * inv
    scaled = grad * gain
    out = inv * (scaled - unit * jnp.mean(scaled * unit, axis=1, keepdims=True))
    return out, jnp.sum(grad * unit, axis=0, keepdims=True)


def second_back_kernel(size, z_ref, cot_ref, gain_ref, res_ref, o0, o1, o2, gr_ref, low_ref, gain_out):
    grad, gain_grad = norm_back(res_ref[...], gain_ref[...], sum_pieces((o0, o1, o2)))
    grad = grad + my_rows(z_ref, cot_ref, res_ref.shape[0])
    gr_ref[...] = grad
    low_ref[...] = grad.astype(bf16)
    gain_out[...] = to_abs(z_ref[1], size, gain_grad)


def first_back_kernel(size, z_ref, x_ref, gain_ref, gr_ref, o0, o1, o2, out_ref):
    x = my_rows(z_ref, x_ref, gr_ref.shape[0])
    grad, _ = norm_back(x, gain_ref[...], sum_pieces((o0, o1, o2)))
    out_ref[...] = to_abs(z_ref[1], size, gr_ref[...] + grad).astype(bf16)


def block_out_kernel(size, z_ref, res_ref, o0, o1, o2, out_ref):
    out_ref[...] = to_abs(z_ref[1], size, res_ref[...] + sum_pieces((o0, o1, o2))).astype(bf16)


def ffn_kernel(groups, first, last, *refs):
    refs = list(refs)

    def take(n):
        taken = refs[:n]
        del refs[:n]
        return taken

    (z_ref,) = take(1)
    if first:
        pieces = take(4)
    else:
        s_any, in_grad = take(2)
    (cot_any,) = take(1)
    s_ref, cot_ref, pre_ref, back_ref, w_ref, acc_grad, sems, out_sems = refs[-8:]
    del refs[-8:]
    n_outs = 2 * groups + (4 if last else 1 + first)
    outs = refs[-n_outs:]
    del refs[-n_outs:]
    per = len(refs) // groups
    rows, width = w_ref.shape[1] // 4, back_ref.shape[1]
    copies = []

    def load(src, dst):
        copy = pltpu.make_async_copy(src, dst, sems.at[len(copies)])
        copy.start()
        copies.append(copy)
        return copy

    held = []
    if not first:
        held.append(load(s_any, s_ref))
    held.append(load(cot_any, cot_ref))
    landing = []
    for g in range(groups):
        at, marks = 0, []
        for piece in refs[g * per : (g + 1) * per]:
            marks.append((at, load(piece, w_ref.at[g, pl.ds(at, piece.shape[0])])))
            at += piece.shape[0]
        landing.append(marks)
    if not first:
        sums = load(in_grad, acc_grad)
    if first:
        assemble_kernel(z_ref, *pieces, s_ref)
    for copy in held:
        copy.wait()
    stores = []

    def store(src, dst):
        copy = pltpu.make_async_copy(src, dst, out_sems.at[len(stores)])
        copy.start()
        stores.append(copy)

    if first:
        store(s_ref, outs[2 * groups])
    for g in range(groups):
        ggu_ref, mid_ref = outs[2 * g : 2 * g + 2]
        for i in range(4):
            at = slice(i * rows, (i + 1) * rows)
            await_rows(landing[g], (i + 1) * rows)
            pre = nn(s_ref[:, at], w_ref[g, at, : 2 * width])
            back = nn(cot_ref[:, at], w_ref[g, at, 2 * width :])
            if i == 0:
                pre_ref[...] = pre
                back_ref[...] = back
            else:
                pre_ref[...] += pre
                back_ref[...] += back
        for c in range(0, width, 128):
            gate, up = pre_ref[:, c : c + 128], pre_ref[:, width + c : width + c + 128]
            back = back_ref[:, c : c + 128]
            gelu_gate, slope = gelu_pair(gate)
            mid_ref[:, c : c + 128] = (gelu_gate * up).astype(bf16)
            ggu_ref[:, c : c + 128] = (back * up * slope).astype(bf16)
            ggu_ref[:, width + c : width + c + 128] = (back * gelu_gate).astype(bf16)
        if g == 0 and not first:
            sums.wait()
        for i in range(4):
            at = slice(i * rows, (i + 1) * rows)
            grad = nt(ggu_ref[...], w_ref[g, at, : 2 * width])
            if first and g == 0:
                acc_grad[:, at] = grad
            else:
                acc_grad[:, at] += grad
            if g == groups - 1 and not last:
                cols = pl.ds(i * rows, rows)
                store(acc_grad.at[:, cols], outs[-1].at[:, cols])
    if last:
        split_rows(z_ref, acc_grad, outs[2:6])
    for copy in stores:
        copy.wait()


def ffn_out_kernel(counts, z_ref, *refs):
    groups = len(counts)
    mids, refs = refs[:groups], refs[groups:]
    own, pass_part, both, w_ref, total_ref, sems = refs[-6:]
    pieces, width = list(refs[:-6]), mids[0].shape[1]
    copies, ends = [], []
    for g in range(groups):
        at = 0
        for piece in [pieces.pop(0) for _ in range(counts[g])]:
            copy = pltpu.make_async_copy(
                piece.at[:, pl.ds(2 * width, width)], w_ref.at[g, pl.ds(at, piece.shape[0])],
                sems.at[len(copies)],
            )
            copy.start()
            copies.append(copy)
            at += piece.shape[0]
        ends.append(len(copies))
    rows = w_ref.shape[1] // 4
    for g in range(groups):
        for copy in copies[ends[g] - counts[g] : ends[g]]:
            copy.wait()
        for i in range(4):
            at = slice(i * rows, (i + 1) * rows)
            out = nt(mids[g][...], w_ref[g, at, :])
            total_ref[:, at] = out if g == 0 else total_ref[:, at] + out
    count = own.shape[0]
    split_rows(
        z_ref, total_ref,
        [own, both.at[pl.ds(count, count)], pass_part, both.at[pl.ds(0, count)]],
    )


def grads_out_kernel(sides, *refs):
    lefts, rights, out = refs[:sides], refs[sides : 2 * sides], refs[2 * sides]
    held, sems = refs[2 * sides + 1 :]
    step = held.shape[0] // 2
    stores = []
    for part in range(2):
        rows, at = slice(part * step, (part + 1) * step), 0
        for left, right in zip(lefts, rights):
            width = right.shape[1]
            held[rows, at : at + width] = tn(left[:, rows], right[...]).astype(bf16)
            at += width
        copy = pltpu.make_async_copy(
            held.at[pl.ds(part * step, step)], out.at[pl.ds(part * step, step)], sems.at[part]
        )
        copy.start()
        stores.append(copy)
    for copy in stores:
        copy.wait()


def grads_own_kernel(sides, room, *refs):
    lefts, rights = refs[:sides], refs[sides : 2 * sides]
    got_any, own, x_top, y_bot, send_x, send_y = refs[2 * sides : 2 * sides + 6]
    got, grads, low, sems = refs[2 * sides + 6 :]
    q = x_top.shape[0]
    loads = [
        pltpu.make_async_copy(
            got_any.at[pl.ds(part * 4 * q, 4 * q)], got.at[pl.ds(part * 4 * q, 4 * q)], sems.at[part]
        )
        for part in range(2)
    ]
    for copy in loads:
        copy.start()
    stores = []

    def store(src, row, count, dst, to):
        copy = pltpu.make_async_copy(
            src.at[pl.ds(row * q, count * q)], dst.at[pl.ds(to * q, count * q)],
            sems.at[2 + len(stores)],
        )
        copy.start()
        stores.append(copy)

    for part in range(2):
        rows, at = slice(part * 4 * q, (part + 1) * 4 * q), 0
        loads[part].wait()
        for left, right in zip(lefts, rights):
            cols = slice(at, at + right.shape[1])
            at += right.shape[1]
            grads[rows, cols] = tn(left[:, rows], right[...]) + got[rows, cols].astype(f32)
        if part == 0:
            low[:q, :] = grads[3 * q : 4 * q, :].astype(bf16)
            store(grads, 0, 2, own, 0)
            store(grads, 2, 1, x_top, 0)
            store(low, 0, 1, send_x, room + 1)
        else:
            low[q : 2 * q, :] = grads[4 * q : 5 * q, :].astype(bf16)
            low[2 * q :, :] = grads[6 * q :, :].astype(bf16)
            store(low, 1, 1, send_y, room + 1)
            store(grads, 5, 1, y_bot, 0)
            store(low, 2, 1, send_y, room)
            store(low, 3, 1, send_x, room)
    for copy in stores:
        copy.wait()


def relay_kernel(groups, has_next, *refs):
    refs = list(refs)
    out_x, out_y = refs[-2:]
    at = 0
    for _ in range(groups):
        x_top, y_bot, got_x, got_y = refs[:4]
        del refs[:4]
        q, cols = x_top.shape[0], slice(at, at + x_top.shape[1])
        out_x[:q, cols] = (x_top[...] + got_y[:, cols].astype(f32)).astype(bf16)
        out_y[:q, cols] = (y_bot[...] + got_x[:, cols].astype(f32)).astype(bf16)
        at += x_top.shape[1]
    at = 0
    for _ in range(has_next):
        send_x, send_y = refs[:2]
        del refs[:2]
        cols = slice(at, at + send_x.shape[1])
        out_x[q:, cols] = send_x[...]
        out_y[q:, cols] = send_y[...]
        at += send_x.shape[1]


def joined(own, got_x, got_y, last_x, last_y, at, cols):
    q = last_x.shape[0]
    top = own[:q, at] + got_y[:, cols].astype(f32) + last_x[:, cols].astype(f32)
    bottom = own[q:, at] + got_x[:, cols].astype(f32) + last_y[:, cols].astype(f32)
    return jnp.concatenate([top, bottom], axis=0)


def join_ffn_kernel(*refs):
    gate_ref, up_ref, down_ref = refs[-3:]
    for c in range(chunk_count):
        parts = refs[5 * c : 5 * c + 5]
        width = parts[0].shape[1] // 3
        at = slice(c * width, (c + 1) * width)
        gate, up, down = [slice(k * width, (k + 1) * width) for k in range(3)]
        gate_ref[:, at] = joined(*parts, gate, gate)
        up_ref[:, at] = joined(*parts, up, up)
        down_ref[:, at] = joined(*parts, down, down)


def add_kernel(a_ref, b_ref, out_ref):
    out_ref[...] = (a_ref[...].astype(f32) + b_ref[...].astype(f32)).astype(out_ref.dtype)


def small_kernel(units, sums_ref, by_x, by_y, across, taps_ref, bias_ref, rate_ref, input_ref, decay_ref, one_ref, two_ref):
    total = (sums_ref[...] + by_x[...]) + (by_y[...] + across[...])
    heads, taps, _ = taps_ref.shape
    for h in range(heads):
        cols = slice(h * units, (h + 1) * units)
        taps_ref[h] = total[8 : 8 + taps, cols]
        bias_ref[h : h + 1, :] = total[8 + taps : 9 + taps, cols]
        rate_ref[h : h + 1, :] = total[1:2, cols]
        input_ref[h : h + 1, :] = total[2:3, cols]
        decay_ref[h : h + 1, :] = total[0:1, cols]
    wide = total.shape[1]
    for k in range(4):
        one_ref[k * wide : (k + 1) * wide] = total[16 + k]
        two_ref[k * wide : (k + 1) * wide] = total[20 + k]


def last_kernel(units, z_ref, *refs):
    x_ins, block_ins, gate_ins, small_ins = refs[:5], refs[5:9], refs[9:11], refs[11:15]
    x_ref, block_ref, rate_ref, input_ref = refs[15:19]
    join_x_kernel(*x_ins, x_ref)
    assemble_kernel(z_ref, *block_ins, block_ref)
    gate_join_kernel(z_ref, *gate_ins, rate_ref, input_ref)
    small_kernel(units, *small_ins, *refs[19:])


def gate_join_kernel(z_ref, mine_ref, other_ref, rate_ref, input_ref):
    pairs, _, units, _ = mine_ref.shape
    core = z_ref[1] % 2
    for src, head in ((mine_ref, core), (other_ref, 1 - core)):
        for p in range(pairs):
            whole = jnp.concatenate([src[p, z_ref[0] ^ owner] for owner in range(4)], axis=0)
            rate_ref[2 * p + head] = whole[:, :units].T
            input_ref[2 * p + head] = whole[:, units:].T


def relay_mixed_kernel(x_top, y_bot, got_x, got_y, send_x, send_y, out_x, out_y):
    q, width = x_top.shape[0], out_x.shape[1]
    for k in range(x_top.shape[1] // width):
        rows, cols = slice(k * q, (k + 1) * q), slice(k * width, (k + 1) * width)
        out_x[rows, :] = (x_top[:, cols] + got_y[:, cols].astype(f32)).astype(bf16)
        out_y[rows, :] = (y_bot[:, cols] + got_x[:, cols].astype(f32)).astype(bf16)
    out_x[(k + 1) * q :, :] = send_x[...]
    out_y[(k + 1) * q :, :] = send_y[...]


def join_yo_kernel(yo_own, yo_got_x, yo_got_y, y_x, y_y, o_x, o_y, y_ref, out_ref):
    width = y_ref.shape[0]
    first, second = slice(0, width), slice(width, 2 * width)
    y_ref[...] = joined(yo_own, yo_got_x[:, first], yo_got_y[:, first], y_x, y_y, first, first).T
    out_ref[...] = joined(
        yo_own, yo_got_x[:, second], yo_got_y[:, second], o_x, o_y, second, first
    ).T


def join_x_kernel(own, got_x, got_y, last_x, last_y, out_ref):
    cols = slice(0, out_ref.shape[0])
    out_ref[...] = joined(own, got_x, got_y, last_x, last_y, cols, cols).T


def exchange(v, axis, size, bit):
    return lax.ppermute(v, axis, [(i, i ^ bit) for i in range(size)])


def tie(*values):
    return lax.optimization_barrier(values)


def along(size, bit, v):
    return exchange(v, "dp", 8, bit) if size == 8 else v


def move(size, send_x, send_y):
    return along(size, 2, send_x), along(size, 4, send_y)


def gather_all(shard, size):
    mine, bit = shard, 2
    while bit < size:
        mine = jnp.concatenate([mine, exchange(mine, "dp", size, bit)], axis=0)
        bit *= 2
    return [mine], [exchange(mine, "dp", size, 1)]


class Scatter:
    def __init__(self, size, lefts, rights, name):
        self.size, self.name = size, name
        self.lefts, self.rights = lefts, rights
        self.model = lefts[0].shape[1]
        self.width = sum(r.shape[1] for r in rights)

    def halves(self, side):
        tokens = self.lefts[0].shape[0]
        return {i: block((tokens, self.model // 2), 0, side) for i in range(len(self.lefts))}

    def sibling(self, run):
        shape = (self.model // 2, self.width)
        return run(
            partial(grads_out_kernel, len(self.lefts)), [like(shape, bf16)],
            *self.lefts, *self.rights, specs=self.halves(1),
            out_specs=[pl.BlockSpec(memory_space=pl.ANY)],
            scratch=[pltpu.VMEM(shape, bf16), pltpu.SemaphoreType.DMA((2,))],
            name="grads_out_" + self.name,
        )[0]

    def swap(self, out):
        return exchange(out, "dp", self.size, 1)

    def own(self, run, got, room=0):
        q, w = self.model // 16, self.width
        sends = [like(((2 + room) * q, w), bf16)] * 2
        anywhere = pl.BlockSpec(memory_space=pl.ANY)
        specs = self.halves(0)
        specs[2 * len(self.lefts)] = anywhere
        return run(
            partial(grads_own_kernel, len(self.lefts), room),
            [like((2 * q, w), f32), like((q, w), f32), like((q, w), f32)] + sends,
            *self.lefts, *self.rights, got, specs=specs, out_specs=[anywhere] * 5,
            scratch=[
                pltpu.VMEM((8 * q, w), bf16), pltpu.VMEM((8 * q, w), f32), pltpu.VMEM((4 * q, w), bf16),
                pltpu.SemaphoreType.DMA((9,)),
            ],
            name="grads_own_" + self.name,
        )

    def join(self, cut):
        own, x_top, y_bot, from_x, from_y = cut
        q = x_top.shape[0]
        from_x, from_y = from_x[-2 * q :], from_y[-2 * q :]
        total = jnp.concatenate(
            [own, x_top, from_x[q:].astype(f32), from_y[q:].astype(f32), y_bot,
             from_y[:q].astype(f32), from_x[:q].astype(f32)],
            axis=0,
        )
        bit = self.size // 2
        while bit > 1:
            half = total.shape[0] // 2
            total = total[:half] + exchange(total[half:].astype(bf16), "dp", self.size, bit).astype(f32)
            bit //= 2
        return total


def relay(run, cuts, got, base, nexts, name):
    q = cuts[0][1].shape[0]
    width = sum(cut[1].shape[1] for cut in cuts)
    ins, specs, options = [], {}, {}
    for cut in cuts:
        ins += [cut[1], cut[2]]
        for v in got:
            specs[len(ins)] = block((q, v.shape[1]), base, 0)
            ins.append(v)
    if len(nexts) == 1:
        options = dict(
            alias={len(ins): 0, len(ins) + 1: 1}, out_specs=[block((q, width), 0, 0)] * 2
        )
        specs[len(ins)] = specs[len(ins) + 1] = pl.BlockSpec(memory_space=pl.ANY)
    for cut in nexts:
        ins += [cut[3], cut[4]]
    return run(
        partial(relay_kernel, len(cuts), 0 if len(nexts) == 1 else len(nexts)),
        [like((3 * q if nexts else q, width), bf16)] * 2, *ins, specs=specs, name=name, **options,
    )


def to_owner(part):
    return exchange(part, "tensor", 4, 1)


def pass_on(part, got):
    return exchange((part + got.astype(f32)).astype(bf16), "tensor", 4, 2)


class Order:
    def __init__(self):
        self.last = None

    def after(self, *values):
        if self.last is not None:
            values, _ = lax.optimization_barrier((values, self.last))
        return values if len(values) > 1 else values[0]

    def wait(self, *values):
        values = self.after(*values)
        self.last = jax.tree.leaves(values)[0]
        return values

    def run(self, kernel, outs, *args, **options):
        results = call(kernel, outs, *self.after(*args), **options)
        self.last = results[0]
        return results


def spread(piece):
    return exchange(piece, "tensor", 4, 2), exchange(piece, "tensor", 4, 1)


def neighbour(v):
    return exchange(v, "tensor", 4, 1)


def sum_over(v, axis, size, first=1, until=None):
    bit = first
    while bit < (until or size):
        v = v + exchange(v, axis, size, bit)
        bit *= 2
    return v


def sum_low(v, axis, size, first=1, until=None):
    bit = first
    while bit < (until or size):
        low = v.astype(bf16)
        v = low.astype(f32) + exchange(low, axis, size, bit).astype(f32)
        bit *= 2
    return v


def body(
    tokens, segments, first_gain, x_weight, y_weight, conv_weight, conv_bias, rate_weight,
    input_weight, rate_bias, input_bias, decay_logit, out_weight, second_gain, gate_weight,
    up_weight, down_weight, cotangent, dp_size,
):
    count, model = tokens.shape
    heads, _, units = rate_weight.shape
    chan = heads * units
    pairs = heads // 2
    taps = conv_weight.shape[0]
    hidden_units = gate_weight.shape[1]
    width = hidden_units // chunk_count
    me = lax.axis_index("dp")
    z = lax.axis_index("tensor").astype(jnp.int32)
    ids = jnp.stack([z, me.astype(jnp.int32)])
    part = model // dp_size
    q = model // 16
    rows = count // 4
    size = dp_size
    order = Order()
    after, wait, run = order.after, order.wait, order.run
    anywhere = pl.BlockSpec(memory_space=pl.ANY)
    lane = pl.BlockSpec((count, 128), lambda p: (0, p))
    line = pl.BlockSpec((1, 128), lambda p: (0, p))
    sums_spec = pl.BlockSpec((8, 128), lambda p: (0, p))
    block_spec = pl.BlockSpec((1, 8 * units, 4 * units), lambda p: (p, 0, 0))
    mask_spec = pl.BlockSpec((taps - 1, count, 128), lambda p: (0, 0, 0))
    pair_grid = dict(
        grid=(pairs,), cost_estimate=hint,
        compiler_params=pltpu.CompilerParams(vmem_limit_bytes=60 * MIB),
    )
    split_shapes = [like((rows, model), t) for t in (f32, bf16, f32, bf16)]
    split_specs = [pl.BlockSpec((rows, model), lambda p: (0, 0))] * 4
    total_scratch = [pltpu.VMEM((count, model), f32)]

    def sibling(v):
        return exchange(v, "dp", size, 1)

    def halves(by_x, by_y):
        half = by_x.shape[0] // 2
        lower, upper = move(size, by_y[half:], by_x[:half])
        return upper, lower

    def pieces_of(shard, *got):
        if size == 8:
            return [shard, *got[: len(got) // 2]], list(got[len(got) // 2 :])
        return gather_all(shard, size)

    def assemble(pieces, dtype, name, specs=None):
        return run(
            assemble_kernel, [like((count, model), dtype)], ids, *pieces, scalars=1, specs=specs,
            name=name,
        )[0]

    xs = x_weight.reshape(part, chan)
    x_x, x_y = move(size, xs, xs)
    x_s = sibling(xs)

    def ffn_shard(c):
        cols = block((part, width), 0, c)
        return run(
            shard_kernel, [like((part, 3 * width), bf16)], gate_weight, up_weight, down_weight.T,
            specs={0: cols, 1: cols, 2: cols}, name="shard",
        )[0]

    f0 = ffn_shard(0)
    y_after, out_after = after(y_weight, out_weight)
    yo = jnp.concatenate([y_after.reshape(part, chan), out_after.reshape(chan, part).T], axis=1)
    x_x, x_y, x_s, yo = wait(x_x, x_y, x_s, yo)

    x_top, x_bot = halves(x_x, x_y)
    x_sx, x_sy = sibling(x_x), sibling(x_y)
    x_rel, nf, gain_one, gain_two = run(
        partial(norm_first_kernel, size),
        [like((count, model), bf16)] * 2 + [like((1, model), f32)] * 2,
        ids, tokens, first_gain, second_gain, scalars=1,
        name="norm_first",
    )
    segs = after(segments)
    masks = jnp.stack(
        [
            jnp.concatenate([jnp.full((lag,), -1, jnp.int32), segs[:-lag]]) == segs
            for lag in range(1, taps)
        ]
    ).astype(f32)
    masks = jnp.broadcast_to(masks[:, :, None], (taps - 1, count, 128))
    taps_flat = conv_weight.reshape(taps, chan)
    bias_flat = conv_bias.reshape(1, chan)
    rate_flat, input_flat = rate_bias.reshape(1, chan), input_bias.reshape(1, chan)
    decay_flat = decay_logit.reshape(1, chan)
    masks, taps_flat, bias_flat, rate_flat, input_flat, decay_flat, x_top, x_bot, x_sx, x_sy = wait(
        masks, taps_flat, bias_flat, rate_flat, input_flat, decay_flat, x_top, x_bot, x_sx, x_sy
    )
    yo_x, yo_y = move(size, *after(yo, yo))
    x_st, x_sb = sibling(x_top), sibling(x_bot)
    x_st, x_sb = wait(x_st, x_sb)
    own_x, sib_x = pieces_of(xs, x_x, x_y, x_top, x_bot, x_s, x_sx, x_sy, x_st, x_sb)
    all_x = own_x + sib_x
    x_branch, conv_low = run(
        branch_kernel, [like((count, chan), f32), like((count, chan), bf16)],
        nf, taps_flat, bias_flat, masks, *all_x,
        specs={4 + i: anywhere for i in range(len(all_x))},
        scratch=[pltpu.VMEM((model, chan), bf16), pltpu.SemaphoreType.DMA((len(all_x),))],
        name="branch",
    )
    conv2, conv1 = spread(conv_low)
    yo_s = sibling(after(yo))
    f1 = ffn_shard(1)
    (blocks,) = run(
        blocks_kernel, [like((pairs, 8 * units, 4 * units), bf16)], ids,
        rate_weight.transpose(0, 2, 1), input_weight.transpose(0, 2, 1),
        scalars=1, name="gate_blocks",
    )
    conv2, conv1, yo_x, yo_y, yo_s = wait(conv2, conv1, yo_x, yo_y, yo_s)
    conv3 = neighbour(conv2)
    yo_top, yo_bot = halves(yo_x, yo_y)
    yo_sx, yo_sy = sibling(yo_x), sibling(yo_y)
    (cot_rel,) = run(
        partial(to_rel_kernel, size), [like((count, model), bf16)], ids, cotangent, scalars=1,
        name="cotangent",
    )
    conv3, yo_top, yo_bot, yo_sx, yo_sy = wait(conv3, yo_top, yo_bot, yo_sx, yo_sy)
    conv = [conv_low, conv1, conv2, conv3]
    f0_x, f0_y = move(size, *after(f0, f0))
    f0_s = sibling(after(f0))
    yo_st, yo_sb = sibling(yo_top), sibling(yo_bot)
    rate, entry, hidden = pl.pallas_call(
        forward_scan_kernel,
        in_specs=[lane] * 4 + [block_spec] + [line] * 3 + [mask_spec],
        out_specs=[lane] * 3,
        out_shape=[like((count, chan), f32)] * 3,
        name="forward_scan",
        **pair_grid,
    )(*conv, blocks, rate_flat, input_flat, decay_flat, masks)
    order.last = rate
    yo_st, yo_sb, f0_s, hidden = wait(yo_st, yo_sb, f0_s, hidden)
    own_yo, sib_yo = pieces_of(yo, yo_x, yo_y, yo_top, yo_bot, yo_s, yo_sx, yo_sy, yo_st, yo_sb)
    all_yo = own_yo + sib_yo
    y_branch, mixed, *parts = run(
        mix_kernel,
        [like((count, chan), f32), like((count, chan), bf16)] + split_shapes,
        ids, nf, hidden, *all_yo, scalars=1,
        specs={3 + i: anywhere for i in range(len(all_yo))},
        scratch=total_scratch
        + [pltpu.VMEM((2, model, chan), bf16), pltpu.SemaphoreType.DMA((2 * len(all_yo),))],
        name="mix",
    )
    got3 = to_owner(parts[3])
    f1_x, f1_y = move(size, f1, after(f1))
    got3, f0_x, f0_y = wait(got3, f0_x, f0_y)
    (low,) = run(add_kernel, [like((rows, model), bf16)], parts[2], got3, name="first_add")
    got2, got1 = exchange(low, "tensor", 4, 2), to_owner(after(parts[1]))
    f0_sx = sibling(f0_x)
    got2, got1, f1_x, f1_y, f0_sx = wait(got2, got1, f1_x, f1_y, f0_sx)
    f0_far, f1_far = along(size, 2, after(f0_y)), along(size, 4, f1_x)
    f1_sx, f1_sy, f0_sy = sibling(f1_x), sibling(f1_y), sibling(after(f0_y))
    residual, second_rows = run(
        norm_second_kernel, [like((rows, model), f32), like((rows, model), bf16)],
        ids, x_rel, gain_two, parts[0], got1, got2, scalars=1, name="norm_second",
    )
    second_rows, f1_sx, f1_sy, f0_sy = wait(second_rows, f1_sx, f1_sy, f0_sy)
    sec2, sec1 = spread(second_rows)
    f2 = ffn_shard(2)
    sec2, sec1 = wait(sec2, sec1)
    sec3 = neighbour(sec2)
    sec3, f0_far, f1_far = wait(sec3, f0_far, f1_far)
    f2_x, f2_y = move(size, *after(f2, f2))
    f0_sf, f1_sf, f1_s = sibling(f0_far), sibling(f1_far), sibling(after(f1))
    f0_sf, f1_sf, f1_s = wait(f0_sf, f1_sf, f1_s)
    f2_s = sibling(after(f2))

    def ffn(left, groups, sums, first, last, name):
        outs = [like((count, 2 * width), bf16), like((count, width), bf16)] * len(groups)
        out_specs = [full(v) for v in outs]
        if first:
            outs.append(like((count, model), bf16))
            out_specs.append(anywhere)
        if last:
            outs += split_shapes
            out_specs += [full(v) for v in split_shapes]
        else:
            outs.append(like((count, model), f32))
            out_specs.append(anywhere)
        weights = sum([own + sib for own, sib in groups], [])
        scratch = [
            pltpu.VMEM((count, model), bf16),
            pltpu.VMEM((count, model), bf16),
            pltpu.VMEM((count, 2 * width), f32),
            pltpu.VMEM((count, width), f32),
            pltpu.VMEM((len(groups), model, 3 * width), bf16),
            pltpu.VMEM((count, model), f32),
            pltpu.SemaphoreType.DMA((len(weights) + 3,)),
            pltpu.SemaphoreType.DMA((5,)),
        ]
        ins = [ids, *left, *sums, cot_rel, *weights]
        at = 1 + len(left) * first
        return run(
            partial(ffn_kernel, len(groups), first, last), outs, *ins, scalars=1, scratch=scratch,
            specs={i: anywhere for i in range(at, len(ins))}, out_specs=out_specs, name=name,
        )

    groups = [
        pieces_of(f0, f0_x, f0_y, f0_far, f0_s, f0_sx, f0_sy, f0_sf),
        pieces_of(f1, f1_x, f1_y, f1_far, f1_s, f1_sx, f1_sy, f1_sf),
    ]
    a, mid0, c, mid1, second, *sums = ffn(
        [second_rows, sec1, sec2, sec3], groups, [], True, False, "ffn_01"
    )
    b, d = mid0, mid1
    s0 = Scatter(size, [second, cot_rel], [a, b], "ffn_0")
    s1 = Scatter(size, [second, cot_rel], [c, d], "ffn_1")
    s0_out = s0.sibling(run)
    s0_out, f2_s, f2_x, f2_y = wait(s0_out, f2_s, f2_x, f2_y)
    f2_top, f2_bot = halves(f2_x, f2_y)
    f2_sx, f2_sy = sibling(f2_x), sibling(f2_y)
    s0_swap = s0.swap(s0_out)
    s1_out = s1.sibling(run)
    f2_sx, f2_sy, s0_swap = wait(f2_sx, f2_sy, s0_swap)
    s0_cut = s0.own(run, s0_swap)
    f2_top, f2_bot, s0_send = wait(f2_top, f2_bot, tuple(s0_cut[3:]))
    f2_st, f2_sb = sibling(f2_top), sibling(f2_bot)
    f2_st, f2_sb = wait(f2_st, f2_sb)
    s0_got = move(size, *after(*s0_send))
    s1_swap = s1.swap(after(s1_out))
    groups.append(pieces_of(f2, f2_x, f2_y, f2_top, f2_bot, f2_s, f2_sx, f2_sy, f2_st, f2_sb))
    a, b, *grad_parts = ffn([second], groups[2:], sums, False, True, "ffn_2")
    mid2 = b
    s2 = Scatter(size, [second, cot_rel], [a, b], "ffn_2")
    grad_parts, s1_swap = wait(tuple(grad_parts), s1_swap)

    got3, got1 = to_owner(grad_parts[3]), to_owner(grad_parts[1])
    s1_cut = s1.own(run, s1_swap)
    s2_out = s2.sibling(run)
    got3, s0_got, s2_out, s1_send = wait(got3, s0_got, s2_out, tuple(s1_cut[3:]))
    got2 = pass_on(grad_parts[2], got3)
    s1_got = move(size, *s1_send)
    s2_swap = s2.swap(s2_out)
    lists = [own + sib for own, sib in groups]
    ins = [ids, mid0, mid1, mid2, *sum(lists, [])]
    out_parts = run(
        partial(ffn_out_kernel, [len(v) for v in lists]),
        [like((rows, model), f32)] * 2 + [like((2 * rows, model), bf16)], *ins, scalars=1,
        specs={i: anywhere for i in range(4, len(ins))},
        scratch=[
            pltpu.VMEM((chunk_count, model, width), bf16), pltpu.VMEM((count, model), f32),
            pltpu.SemaphoreType.DMA((len(ins),)),
        ],
        name="ffn_out",
    )
    got2, got1, s2_swap = wait(got2, got1, s2_swap)
    grad_res, rec_rows, second_gain = run(
        partial(second_back_kernel, size),
        [like((rows, model), f32), like((rows, model), bf16), like((1, model), f32)],
        ids, cot_rel, gain_two, residual, grad_parts[0], got1, got2, scalars=1, micros=6, name="second_back",
    )
    rec2, rec1 = spread(rec_rows)
    s2_cut = s2.own(run, s2_swap, 1)
    sends = relay(run, [s0_cut], s0_got, 0, [s2_cut], "relay_0")
    rec2, rec1, s1_got, sends = wait(rec2, rec1, s1_got, tuple(sends))
    rec3 = neighbour(rec2)
    slot = move(size, *sends)
    rec3 = wait(rec3)
    out_got = neighbour(after(out_parts[2]))

    whole = pl.BlockSpec((count, model), lambda p: (0, 0))
    piece = pl.BlockSpec((rows, model), lambda p: (0, 0))
    gate_spec = pl.BlockSpec((1, 4, units, 2 * units), lambda p: (p, 0, 0, 0))
    gate_half = like((pairs, 4, units, 2 * units), bf16)
    grad_rec, grad_y, direct, h1, h2, h3, gate_mine, gate_theirs, scan_sums = pl.pallas_call(
        partial(backward_scan_kernel, len(all_yo)),
        in_specs=[smem] + [piece] * 4
        + [pl.BlockSpec((v.shape[0], 128), lambda p: (0, pairs + p)) for v in all_yo] + [lane] * 4
        + [block_spec, line, lane, mask_spec] + [lane] * 3,
        out_specs=[whole, lane, lane, lane, lane, lane, gate_spec, gate_spec, sums_spec],
        out_shape=[like((count, model), bf16)]
        + [like((count, chan), t) for t in (bf16, f32, bf16, f32, bf16)]
        + [gate_half, gate_half, like((8, chan), f32)],
        name="backward_scan",
        **pair_grid,
    )(
        *after(ids, rec_rows, rec1, rec2, rec3, *all_yo, *conv, blocks, decay_flat, y_branch, masks),
        rate, entry, hidden,
    )
    order.last = grad_rec
    out_got, h1, h2, h3 = wait(out_got, h1, h2, h3)
    got3 = to_owner(h3)
    gate_got = sibling(gate_theirs)
    syo = Scatter(size, [nf, grad_rec], [grad_y, mixed], "yo")
    syo_out = syo.sibling(run)
    s1_send = relay(run, [s1_cut], s1_got, 0, [], "relay_1")
    got3, syo_out, gate_got, s1_send = wait(got3, syo_out, gate_got, tuple(s1_send))
    got2, got1 = pass_on(h2, got3), to_owner(after(h1))
    (gate_sum,) = run(add_kernel, [gate_half], gate_mine, gate_got, name="gate_add")
    (out_low,) = run(
        add_kernel, [like((rows, model), bf16)], out_parts[1], out_got,
        specs={1: block((rows, model), 0, 0)}, name="out_add",
    )
    got2, got1, slot, out_low = wait(got2, got1, slot, out_low)
    out_got2 = exchange(out_low, "tensor", 4, 2)
    s1_last = move(size, *after(*s1_send))
    syo_swap = syo.swap(after(syo_out))
    gate_got = along(size, 2, after(gate_sum))
    whole_row = pl.BlockSpec((1, model), lambda p: (0, 0))
    grad_x, conv_sums, first_gain, *first_parts = pl.pallas_call(
        partial(conv_back_kernel, size, len(all_x)),
        in_specs=[smem] + [lane] * 4 + [pl.BlockSpec((taps, 128), lambda p: (0, p)), mask_spec, lane]
        + [whole] + [anywhere] * (2 * len(all_x)),
        out_specs=[lane, sums_spec, whole_row] + split_specs,
        out_shape=[like((count, chan), bf16), like((8, chan), f32), like((1, model), f32)]
        + split_shapes,
        scratch_shapes=total_scratch
        + [
            pltpu.VMEM((model, 2 * chan), bf16),
            pltpu.VMEM((count, 2 * chan), bf16),
            pltpu.SemaphoreType.DMA((2 * len(all_x),)),
        ],
        name="conv_back",
        **pair_grid,
    )(*after(ids, direct, got1, got2, x_branch, taps_flat, masks, grad_y, x_rel, *all_x, *all_yo))
    order.last = grad_x
    first_parts, syo_swap, out_got2 = wait(tuple(first_parts), syo_swap, out_got2)
    got3 = to_owner(first_parts[3])
    sx = Scatter(size, [nf], [grad_x], "x")
    sx_out = sx.sibling(run)
    syo_cut = syo.own(run, syo_swap)
    s2_send = relay(run, [s2_cut], slot, 1, [], "relay_2")
    got3, sx_out, yo_send, s1_last, gate_got, s2_send = wait(
        got3, sx_out, tuple(syo_cut[3:]), s1_last, gate_got, tuple(s2_send)
    )
    got2, got1 = pass_on(first_parts[2], got3), to_owner(after(first_parts[1]))
    sx_swap = sx.swap(sx_out)
    yo_got = move(size, *yo_send)
    got2, got1, sx_swap, yo_got = wait(got2, got1, sx_swap, yo_got)
    (tokens_rows,) = run(
        partial(first_back_kernel, size), [like((rows, model), bf16)],
        ids, x_rel, gain_one, grad_res, first_parts[0], got1, got2, scalars=1, name="first_back",
    )
    gains = jnp.concatenate([first_gain, second_gain], axis=0)
    tok2, tok1 = spread(tokens_rows)
    gains = sum_over(after(gains), "tensor", 4, 1, 2)
    s2_last = move(size, *after(*s2_send))
    sx_cut = sx.own(run, sx_swap)
    specs = {k: block((q, 2 * chan), 0, 0) for k in (2, 3)}
    mixed_sends = run(
        relay_mixed_kernel, [like((4 * q, chan), bf16)] * 2, syo_cut[1], syo_cut[2], *yo_got,
        *sx_cut[3:], specs=specs, name="relay_3",
    )
    (block_rows,) = run(
        partial(block_out_kernel, size), [like((rows, model), bf16)],
        ids, residual, out_parts[0], out_got, out_got2, scalars=1,
        specs={3: block((rows, model), 1, 0)}, name="block_out",
    )
    (gate_sum,) = run(add_kernel, [gate_half], gate_sum, gate_got, name="gate_add")
    tok2, tok1, s2_last, gains, mixed_sends = wait(tok2, tok1, s2_last, gains, tuple(mixed_sends))
    tok3 = neighbour(tok2)
    slot3 = move(size, *mixed_sends)
    block2 = exchange(after(block_rows), "tensor", 4, 2)
    gains = sum_over(gains, "tensor", 4, 2)
    if size == 8:
        ins, specs = [], {}
        for cut, (got, base), last in (
            (s0_cut, (s0_got, 0), slot), (s1_cut, (s1_got, 0), s1_last), (s2_cut, (slot, 1), s2_last)
        ):
            ins.append(cut[0])
            for v, at in ((got[0], base + 1), (got[1], base + 1), (last[0], 0), (last[1], 0)):
                specs[len(ins)] = block((q, v.shape[1]), at, 0)
                ins.append(v)
        gate_share, up_share, down_share = run(
            join_ffn_kernel,
            [like((part, hidden_units), f32)] * 3,
            *ins, specs=specs, name="join_ffn",
        )
    else:
        shares = [s0.join(s0_cut), s1.join(s1_cut), s2.join(s2_cut)]
        gate_share, up_share, down_share = [
            jnp.concatenate([v[:, k * width : (k + 1) * width] for v in shares], axis=1)
            for k in range(3)
        ]
    tok3, gains, slot3, block2 = wait(tok3, gains, slot3, block2)
    small = jnp.concatenate([scan_sums, conv_sums, gains.reshape(8, chan)], axis=0)
    small = sum_over(small, "dp", size, 1, 2)
    block13 = neighbour(jnp.concatenate([block_rows, block2], axis=0))
    gate_got = along(size, 4, after(gate_sum))
    x_last = move(size, *relay(run, [sx_cut], slot3, 2, [], "relay_4"))
    yo_ins = [syo_cut[0], *yo_got, *slot3, *slot3]
    if size == 8:
        specs = {1: block((q, 2 * chan), 1, 0), 2: block((q, 2 * chan), 1, 0)}
        for k, at in enumerate((0, 0, 1, 1)):
            specs[3 + k] = block((q, chan), at, 0)
        y_share, out_share = run(
            join_yo_kernel, [like((chan, part), f32)] * 2, *yo_ins, specs=specs, name="join_yo"
        )
    tokens_grad = assemble([tokens_rows, tok1, tok2, tok3], f32, "tokens_grad_all")
    (gate_sum,) = run(
        add_kernel, [like(gate_half.shape, f32)], gate_sum, wait(gate_got), name="gate_add"
    )
    x_last, block13, small, gate_sum = wait(x_last, block13, small, gate_sum)
    block_ins = [block_rows, block13, block2, block13]
    block_specs = {2: block((rows, model), 0, 0), 4: block((rows, model), 1, 0)}
    if size == 8:
        by_x, by_y, across = [exchange(small, "dp", size, bit) for bit in (2, 4, 6)]
        gate_got = sibling(gate_sum)
        gate_got, by_x, by_y, across = wait(gate_got, by_x, by_y, across)
        ins = [ids, sx_cut[0], *slot3, *x_last, *block_ins, gate_sum, gate_got, small, by_x, by_y, across]
        specs = {k: block((q, chan), 3 if k < 4 else 0, 0) for k in range(2, 6)}
        specs.update({6 + k: v for k, v in ((1, block_specs[2]), (3, block_specs[4]))})
        head_like, gate_like = like((heads, units), f32), like((heads, units, 4 * units), f32)
        (
            x_share, block_out, rate_grad, input_grad, taps_grad, bias_grad, rate_b_grad,
            input_b_grad, decay_grad, one_grad, two_grad,
        ) = run(
            partial(last_kernel, units),
            [like((chan, part), f32), like((count, model), bf16), gate_like, gate_like]
            + [like((heads, taps, units), f32)] + [head_like] * 4 + [like((model,), f32)] * 2,
            *ins, scalars=1, specs=specs, name="last",
        )
        rate_grad, input_grad = rate_grad.transpose(0, 2, 1), input_grad.transpose(0, 2, 1)
        taps_grad = taps_grad.transpose(1, 0, 2)
    else:
        block_out = assemble(block_ins, bf16, "block_out_all", block_specs)
        small = sum_over(small, "dp", size, 2)
        taps_grad = small[8 : 8 + taps].reshape(taps, heads, units)
        bias_grad, rate_b_grad, input_b_grad, decay_grad = [
            small[k].reshape(heads, units) for k in (8 + taps, 1, 2, 0)
        ]
        one_grad, two_grad = small[16:20].reshape(model), small[20:].reshape(model)
        yo_share, x_share = syo.join(syo_cut), sx.join(sx_cut)
        x_share, y_share, out_share = x_share.T, yo_share[:, :chan].T, yo_share[:, chan:].T
        mine = sum_low(gate_mine + sibling(gate_theirs), "dp", size, 2)
        other, core = sibling(mine), me % 2
        gate_sum = jnp.stack(
            [jnp.where(core == 0, mine, other), jnp.where(core == 0, other, mine)], axis=1
        ).reshape(heads, 4, units, 2 * units)
        gate_sum = jnp.concatenate(
            [lax.dynamic_index_in_dim(gate_sum, z ^ k, 1, False) for k in range(4)], axis=1
        )
        rate_grad, input_grad = gate_sum[:, :, :units], gate_sum[:, :, units:]
    x_share = x_share.reshape(heads, units, part).transpose(2, 0, 1)
    y_share = y_share.reshape(heads, units, part).transpose(2, 0, 1)
    return (
        block_out,
        tokens_grad,
        one_grad,
        x_share,
        y_share,
        taps_grad,
        bias_grad,
        rate_grad,
        input_grad,
        rate_b_grad,
        input_b_grad,
        decay_grad,
        out_share.reshape(heads, units, part),
        two_grad,
        gate_share,
        up_share,
        down_share.T,
    )


def solution(mesh):
    return jax.shard_map(
        partial(body, dp_size=mesh.shape["dp"]),
        mesh=mesh,
        in_specs=(
            P("dp", None),
            P("dp"),
            P(),
            P("dp", None, "tensor"),
            P("dp", None, "tensor"),
            P(None, None, "tensor"),
            P(None, "tensor"),
            P(None, None, "tensor"),
            P(None, None, "tensor"),
            P(None, "tensor"),
            P(None, "tensor"),
            P(None, "tensor"),
            P(None, "tensor", "dp"),
            P(),
            P("dp", "tensor"),
            P("dp", "tensor"),
            P("tensor", "dp"),
            P("dp", None),
        ),
        out_specs=(
            P("dp", None),
            P("dp", None),
            P(),
            P("dp", None, "tensor"),
            P("dp", None, "tensor"),
            P(None, None, "tensor"),
            P(None, "tensor"),
            P(None, None, "tensor"),
            P(None, None, "tensor"),
            P(None, "tensor"),
            P(None, "tensor"),
            P(None, "tensor"),
            P(None, "tensor", "dp"),
            P(),
            P("dp", "tensor"),
            P("dp", "tensor"),
            P("tensor", "dp"),
        ),
        check_vma=False,
    )
```

profile of v0, /device:TPU:0, one launch (start us, length us, event | category | flops | bytes accessed | tf_op | source)
XLA Modules:
  0.0 460.5 jit_solution(9174952517606886430)
XLA Ops:
  2.4 2.6 collective-permute-start.1
  6.5 2.4 shard.3.refs_6_.refs_3_
  12.9 2.2 collective-permute-done.1.refs_2_
  19.8 4.1 norm_first.1
  30.8 5.6 %branch.1 = (f32[256,640]{1,0:T(8,128)}, bf16[256,640]{1,0:T(8,128)(2,1)}) custom-call(bf16[256,2560]{1,0:T(8,128)(2,1)} %get-tuple-element.1038.nf_ref.refs_0_, f32[4,640]{1,0:T(4,128)} %reshape.98.taps_ref, f32[1,640]{1,0:T(1,128)} %reshape.99.bias_ref, f32[3,256,128]{2,1,0:T(8,128)} %broadcast_in_dim.2.mask_ref.refs_17_, bf16[320,640]{1,0:T(8,128)(2,1)} %copy.47.refs_0_, ...), custom_call_target="tpu_custom_call" | custom-call | flops 1 | bytes 1 | tf_op jit(solution)/shard_map/branch/pallas_call | solution.py:51
  38.1 2.6 collective-permute-start.9
  40.7 2.5 shard.4.refs_14_.refs_11_
  43.2 2.7 gate_blocks.1.block_ref.refs_14_
  45.9 7.8 %collective-permute-done.10.c1.refs_11_ = bf16[256,640]{1,0:T(8,128)(2,1)S(1)} collective-permute-done((bf16[256,640]{1,0:T(8,128)(2,1)}, bf16[256,640]{1,0:T(8,128)(2,1)S(1)}, u32[]{:S(2)}, u32[]{:S(2)}) %collective-permute-start.10) | collective-permute-done | bytes 327712 | tf_op jit(solution)/shard_map/ppermute | solution.py:742
  53.7 2.4 collective-permute-done.9.c2.refs_12_
  60.5 3.4 cotangent.1.refs_5_.refs_1_.refs_3_.cot_ref
  63.9 5.3 %collective-permute-done.14.c3.refs_13_ = bf16[256,640]{1,0:T(8,128)(2,1)S(1)} collective-permute-done((bf16[256,640]{1,0:T(8,128)(2,1)}, bf16[256,640]{1,0:T(8,128)(2,1)S(1)}, u32[]{:S(2)}, u32[]{:S(2)}) %collective-permute-start.14) | collective-permute-done | bytes 327712 | tf_op jit(solution)/shard_map/ppermute | solution.py:742
  73.1 6.5 %forward_scan.1 = (f32[256,640]{1,0:T(8,128)}, f32[256,640]{1,0:T(8,128)}, f32[256,640]{1,0:T(8,128)}) custom-call(bf16[256,640]{1,0:T(8,128)(2,1)} %get-tuple-element.905.c0.refs_10_, bf16[256,640]{1,0:T(8,128)(2,1)} %copy-done.40, bf16[256,640]{1,0:T(8,128)(2,1)} %copy-done.41, bf16[256,640]{1,0:T(8,128)(2,1)} %copy-done.42, ...), custom_call_target="tpu_custom_call" | custom-call | flops 1 | bytes 1 | tf_op jit(solution)/shard_map/forward_scan/pallas_call | solution.py:1024
  80.5 8.3 %mix.1 = (f32[256,640]{1,0:T(8,128)}, bf16[256,640]{1,0:T(8,128)(2,1)}, f32[64,2560]{1,0:T(8,128)}, bf16[64,2560]{1,0:T(8,128)(2,1)}, f32[64,2560]{1,0:T(8,128)}, /*index=5*/bf16[64,2560]{1,0:T(8,128)(2,1)}) custom-call(s32[2]{0:T(128)} %pad_add_fusion.z_ref.refs_0_, bf16[256,2560]{1,0:T(8,128)(2,1)} %get-tuple-element.1038.nf_ref.refs_0_, ...), custom_call_target="tpu_custom_call" | custom-call | flops 1 | bytes 1 | tf_op jit(solution)/shard_map/mix/pallas_call | solution.py:51
  91.3 9.2 %collective-permute-done.23.refs_7_.refs_4_ = bf16[320,1920]{1,0:T(8,128)(2,1)} collective-permute-done((bf16[320,1920]{1,0:T(8,128)(2,1)S(1)}, bf16[320,1920]{1,0:T(8,128)(2,1)}, u32[]{:S(2)}, u32[]{:S(2)}) %collective-permute-start.23) | collective-permute-done | bytes 1228832 | tf_op jit(solution)/shard_map/ppermute | solution.py:742
  105.1 2.6 collective-permute-start.25
  107.7 18.5 %collective-permute-done.27.refs_15_.refs_12_ = bf16[320,1920]{1,0:T(8,128)(2,1)S(1)} collective-permute-done((bf16[320,1920]{1,0:T(8,128)(2,1)S(1)}, bf16[320,1920]{1,0:T(8,128)(2,1)S(1)}, u32[]{:S(2)}, u32[]{:S(2)}) %collective-permute-start.27) | collective-permute-done | bytes 1228832 | tf_op jit(solution)/shard_map/ppermute | solution.py:742
  129.6 2.8 norm_second.1
  134.7 2.6 collective-permute-start.33
  137.3 2.4 shard.5.refs_4_.refs_19_
  139.7 11.3 %collective-permute-done.34.refs_2_ = bf16[64,2560]{1,0:T(8,128)(2,1)S(1)} collective-permute-done((bf16[64,2560]{1,0:T(8,128)(2,1)}, bf16[64,2560]{1,0:T(8,128)(2,1)S(1)}, u32[]{:S(2)}, u32[]{:S(2)}) %collective-permute-start.34) | collective-permute-done | bytes 327712 | tf_op jit(solution)/shard_map/ppermute | solution.py:742
  152.7 5.1 %collective-permute-done.36.refs_9_.refs_6_ = bf16[320,1920]{1,0:T(8,128)(2,1)} collective-permute-done((bf16[320,1920]{1,0:T(8,128)(2,1)}, bf16[320,1920]{1,0:T(8,128)(2,1)}, u32[]{:S(2)}, u32[]{:S(2)}) %collective-permute-start.36) | collective-permute-done | bytes 1228832 | tf_op jit(solution)/shard_map/ppermute | solution.py:742
  157.8 2.3 collective-permute-done.35.refs_4_
  162.3 2.4 collective-permute-done.40.refs_18_.refs_15_
  168.0 18.6 %ffn_01.1 = (bf16[256,1280]{1,0:T(8,128)(2,1)}, bf16[256,640]{1,0:T(8,128)(2,1)}, bf16[256,1280]{1,0:T(8,128)(2,1)}, bf16[256,640]{1,0:T(8,128)(2,1)}, bf16[256,2560]{1,0:T(8,128)(2,1)}, /*index=5*/f32[256,2560]{1,0:T(8,128)}) custom-call(s32[2]{0:T(128)} %pad_add_fusion.z_ref.refs_0_, bf16[64,2560]{1,0:T(8,128)(2,1)} %get-tuple-element.721.refs_1_, ...), custom_call_target="tpu_custom_call" | custom-call | flops 1 | bytes 1 | tf_op jit(solution)/shard_map/ffn_01/pallas_call | solution.py:51
  186.7 4.6 %grads_out_ffn_0.1 = bf16[1280,1920]{1,0:T(8,128)(2,1)} custom-call(bf16[256,2560]{1,0:T(8,128)(2,1)} %get-tuple-element.871.refs_0_.refs_1_, bf16[256,2560]{1,0:T(8,128)(2,1)} %cotangent.1.refs_5_.refs_1_.refs_3_.cot_ref, bf16[256,1280]{1,0:T(8,128)(2,1)} %get-tuple-element.766.refs_2_, bf16[256,640]{1,0:T(8,128)(2,1)} %get-tuple-element.823.refs_3_.refs_0_), custom_call_target="tpu_custom_call" | custom-call | flops 1 | bytes 1 | tf_op jit(solution)/shard_map/grads_out_ffn_0/pallas_call | solution.py:51
  195.7 4.6 %grads_out_ffn_1.1 = bf16[1280,1920]{1,0:T(8,128)(2,1)} custom-call(bf16[256,2560]{1,0:T(8,128)(2,1)} %get-tuple-element.871.refs_0_.refs_1_, bf16[256,2560]{1,0:T(8,128)(2,1)} %cotangent.1.refs_5_.refs_1_.refs_3_.cot_ref, bf16[256,1280]{1,0:T(8,128)(2,1)} %get-tuple-element.809.refs_2_, bf16[256,640]{1,0:T(8,128)(2,1)} %get-tuple-element.824.refs_3_.refs_1_), custom_call_target="tpu_custom_call" | custom-call | flops 1 | bytes 1 | tf_op jit(solution)/shard_map/grads_out_ffn_1/pallas_call | solution.py:51
  200.4 2.8 collective-permute-done.47.refs_11_.refs_26_
  203.5 7.2 %grads_own_ffn_0.1 = (f32[320,1920]{1,0:T(8,128)}, f32[160,1920]{1,0:T(8,128)}, f32[160,1920]{1,0:T(8,128)}, bf16[320,1920]{1,0:T(8,128)(2,1)}, bf16[320,1920]{1,0:T(8,128)(2,1)}) custom-call(bf16[256,2560]{1,0:T(8,128)(2,1)} %get-tuple-element.871.refs_0_.refs_1_, bf16[256,2560]{1,0:T(8,128)(2,1)} %cotangent.1.refs_5_.refs_1_.refs_3_.cot_ref, ...), custom_call_target="tpu_custom_call" | custom-call | flops 1 | bytes 1 | tf_op jit(solution)/shard_map/grads_own_ffn_0/pallas_call | solution.py:51
  216.3 11.0 %ffn_2.1 = (bf16[256,1280]{1,0:T(8,128)(2,1)}, bf16[256,640]{1,0:T(8,128)(2,1)}, f32[64,2560]{1,0:T(8,128)}, bf16[64,2560]{1,0:T(8,128)(2,1)}, f32[64,2560]{1,0:T(8,128)}, /*index=5*/bf16[64,2560]{1,0:T(8,128)(2,1)}) custom-call(s32[2]{0:T(128)} %pad_add_fusion.z_ref.refs_0_, bf16[256,2560]{1,0:T(8,128)(2,1)} %get-tuple-element.871.refs_0_.refs_1_, ...), custom_call_target="tpu_custom_call" | custom-call | flops 1 | bytes 1 | tf_op jit(solution)/shard_map/ffn_2/pallas_call | solution.py:51
  228.8 7.2 %grads_own_ffn_1.1 = (f32[320,1920]{1,0:T(8,128)}, f32[160,1920]{1,0:T(8,128)}, f32[160,1920]{1,0:T(8,128)}, bf16[320,1920]{1,0:T(8,128)(2,1)}, bf16[320,1920]{1,0:T(8,128)(2,1)}) custom-call(bf16[256,2560]{1,0:T(8,128)(2,1)} %get-tuple-element.871.refs_0_.refs_1_, bf16[256,2560]{1,0:T(8,128)(2,1)} %cotangent.1.refs_5_.refs_1_.refs_3_.cot_ref, ...), custom_call_target="tpu_custom_call" | custom-call | flops 1 | bytes 1 | tf_op jit(solution)/shard_map/grads_own_ffn_1/pallas_call | solution.py:51
  236.0 4.7 %grads_out_ffn_2.1 = bf16[1280,1920]{1,0:T(8,128)(2,1)} custom-call(bf16[256,2560]{1,0:T(8,128)(2,1)} %get-tuple-element.871.refs_0_.refs_1_, bf16[256,2560]{1,0:T(8,128)(2,1)} %cotangent.1.refs_5_.refs_1_.refs_3_.cot_ref, bf16[256,1280]{1,0:T(8,128)(2,1)} %get-tuple-element.873.refs_2_, bf16[256,640]{1,0:T(8,128)(2,1)} %get-tuple-element.874.refs_3_.refs_2_), custom_call_target="tpu_custom_call" | custom-call | flops 1 | bytes 1 | tf_op jit(solution)/shard_map/grads_out_ffn_2/pallas_call | solution.py:51
  240.7 3.0 collective-permute-done.53.refs_2_.refs_1_
  250.5 2.4 collective-permute-start.55
  252.9 9.0 %ffn_out.1 = (f32[64,2560]{1,0:T(8,128)}, f32[64,2560]{1,0:T(8,128)}, bf16[128,2560]{1,0:T(8,128)(2,1)}) custom-call(s32[2]{0:T(128)} %pad_add_fusion.z_ref.refs_0_, bf16[256,640]{1,0:T(8,128)(2,1)} %get-tuple-element.823.refs_3_.refs_0_, bf16[256,640]{1,0:T(8,128)(2,1)} %get-tuple-element.824.refs_3_.refs_1_, ...), custom_call_target="tpu_custom_call" | custom-call | flops 1 | bytes 1 | tf_op jit(solution)/shard_map/ffn_out/pallas_call | solution.py:51
  262.0 4.8 %collective-permute-done.55.o2 = bf16[64,2560]{1,0:T(8,128)(2,1)S(1)} collective-permute-done((bf16[64,2560]{1,0:T(8,128)(2,1)S(1)}, bf16[64,2560]{1,0:T(8,128)(2,1)S(1)}, u32[]{:S(2)}, u32[]{:S(2)}) %collective-permute-start.55) | collective-permute-done | bytes 327712 | tf_op jit(solution)/shard_map/ppermute | solution.py:742
  267.5 3.3 second_back.1
  270.8 2.7 collective-permute-start.58
  273.5 7.2 %grads_own_ffn_2.1 = (f32[320,1920]{1,0:T(8,128)}, f32[160,1920]{1,0:T(8,128)}, f32[160,1920]{1,0:T(8,128)}, bf16[480,1920]{1,0:T(8,128)(2,1)}, bf16[480,1920]{1,0:T(8,128)(2,1)}) custom-call(bf16[256,2560]{1,0:T(8,128)(2,1)} %get-tuple-element.871.refs_0_.refs_1_, bf16[256,2560]{1,0:T(8,128)(2,1)} %cotangent.1.refs_5_.refs_1_.refs_3_.cot_ref, ...), custom_call_target="tpu_custom_call" | custom-call | flops 1 | bytes 1 | tf_op jit(solution)/shard_map/grads_own_ffn_2/pallas_call | solution.py:51
  280.7 3.1 relay_0.1
  289.7 4.7 %collective-permute-done.62.p3 = bf16[64,2560]{1,0:T(8,128)(2,1)} collective-permute-done((bf16[64,2560]{1,0:T(8,128)(2,1)}, bf16[64,2560]{1,0:T(8,128)(2,1)}, u32[]{:S(2)}, u32[]{:S(2)}) %collective-permute-start.62) | collective-permute-done | bytes 327712 | tf_op jit(solution)/shard_map/ppermute | solution.py:742
  294.5 11.1 %backward_scan.1 = (bf16[256,2560]{1,0:T(8,128)(2,1)}, bf16[256,640]{1,0:T(8,128)(2,1)}, f32[256,640]{1,0:T(8,128)}, bf16[256,640]{1,0:T(8,128)(2,1)}, f32[256,6...) custom-call(s32[2]{0:T(128)} %pad_add_fusion.z_ref.refs_0_, ...), custom_call_target="tpu_custom_call" | custom-call | flops 1 | bytes 1 | tf_op jit(solution)/shard_map/backward_scan/pallas_call | solution.py:1166
  305.7 2.5 collective-permute-done.63.b_ref.o1
  308.5 3.9 grads_out_yo.1
  312.4 3.2 relay_1.1
  323.5 8.4 %collective-permute-done.67.r1 = bf16[256,640]{1,0:T(8,128)(2,1)S(1)} collective-permute-done((bf16[256,640]{1,0:T(8,128)(2,1)}, bf16[256,640]{1,0:T(8,128)(2,1)S(1)}, u32[]{:S(2)}, u32[]{:S(2)}) %collective-permute-start.67) | collective-permute-done | bytes 327712 | tf_op jit(solution)/shard_map/ppermute | solution.py:742
  332.7 2.2 collective-permute-start.71
  335.7 2.2 collective-permute-start.74
  340.9 10.7 %conv_back.1 = (bf16[256,640]{1,0:T(8,128)(2,1)}, f32[8,640]{1,0:T(8,128)}, f32[1,2560]{1,0:T(1,128)}, f32[64,2560]{1,0:T(8,128)}, bf16[64,2560]{1,0:T(8,128)(2,...) custom-call(s32[2]{0:T(128)} %pad_add_fusion.z_ref.refs_0_, f32[256,640]{1,0:T(8,128)} %get-tuple-element.956.direct_ref, ...), custom_call_target="tpu_custom_call" | custom-call | flops 1 | bytes 1 | tf_op jit(solution)/shard_map/conv_back/pallas_call | solution.py:1201
  351.6 2.7 collective-permute-start.72
  354.3 2.9 grads_out_x.1
  357.2 5.9 %grads_own_yo.1 = (f32[320,1280]{1,0:T(8,128)}, f32[160,1280]{1,0:T(8,128)}, f32[160,1280]{1,0:T(8,128)}, bf16[320,1280]{1,0:T(8,128)(2,1)}, bf16[320,1280]{1,0:T(8,128)(2,1)}) custom-call(bf16[256,2560]{1,0:T(8,128)(2,1)} %get-tuple-element.1038.nf_ref.refs_0_, bf16[256,2560]{1,0:T(8,128)(2,1)} %get-tuple-element.999.refs_1_, ...), custom_call_target="tpu_custom_call" | custom-call | flops 1 | bytes 1 | tf_op jit(solution)/shard_map/grads_own_yo/pallas_call | solution.py:51
  363.1 3.1 relay_2.1
  371.7 14.0 %collective-permute-done.77.o1 = bf16[64,2560]{1,0:T(8,128)(2,1)S(1)} collective-permute-done((bf16[64,2560]{1,0:T(8,128)(2,1)S(1)}, bf16[64,2560]{1,0:T(8,128)(2,1)S(1)}, u32[]{:S(2)}, u32[]{:S(2)}) %collective-permute-start.77) | collective-permute-done | bytes 327712 | tf_op jit(solution)/shard_map/ppermute | solution.py:742
  388.3 4.1 first_back.1.refs_0_
  394.5 2.7 collective-permute-start.81
  398.7 4.4 grads_own_x.1
  403.1 3.2 relay_3.1
  406.3 2.5 block_out.1.refs_5_
  416.4 8.6 %join_ffn.1 = (f32[320,1920]{1,0:T(8,128)}, f32[320,1920]{1,0:T(8,128)}, f32[320,1920]{1,0:T(8,128)}) custom-call(f32[320,1920]{1,0:T(8,128)} %get-tuple-element.1081.refs_0_, bf16[320,1920]{1,0:T(8,128)(2,1)} %copy-done.14, bf16[320,1920]{1,0:T(8,128)(2,1)} %copy-done.15, bf16[480,1920]{1,0:T(8,128)(2,1)} %copy-done, ...), custom_call_target="tpu_custom_call" | custom-call | flops 1 | bytes 1 | tf_op jit(solution)/shard_map/join_ffn/pallas_call | solution.py:51
  425.0 2.9 collective-permute-done.87
  435.9 3.5 join_yo.1
  439.4 2.9 tokens_grad_all.1
  454.6 5.4 %last.1 = (f32[640,320]{1,0:T(8,128)}, bf16[256,2560]{1,0:T(8,128)(2,1)}, f32[10,64,256]{2,1,0:T(8,128)}, f32[10,64,256]{2,1,0:T(8,128)}, f32[10,4,64]{2,1,0:T(4...) custom-call(s32[2]{0:T(128)} %pad_add_fusion.z_ref.refs_0_, ...), custom_call_target="tpu_custom_call" | custom-call | flops 1 | bytes 1 | tf_op jit(solution)/shard_map/last/pallas_call | solution.py:51
  (385 shorter events, 126.7 us)
Async XLA Ops:
  2.4 12.7 %collective-permute-start.1 = (bf16[320,640]{1,0:T(8,128)(2,1)S(1)}, bf16[320,640]{1,0:T(8,128)(2,1)S(1)}, u32[]{:S(2)}, u32[]{:S(2)}) collective-permute-start(bf16[320,640]{1,0:T(8,128)(2,1)S(1)} %copy.41), channel_id=1, source_target_pairs={{0,16},{4,20},{8,24},{12,28},{16,0},{20,4},{24,8},{28,12},{1,17},{... | collective-permute-start | bytes 1228808 | tf_op jit(solution)/shard_map/ppermute | solution.py:742
  26.6 29.5 %collective-permute-start.11 = (bf16[320,1280]{1,0:T(8,128)(2,1)S(1)}, bf16[320,1280]{1,0:T(8,128)(2,1)S(1)}, u32[]{:S(2)}, u32[]{:S(2)}) collective-permute-start(bf16[320,1280]{1,0:T(8,128)(2,1)S(1)} %pad_maximum_fusion.refs_0_.refs_10_), channel_id=1, source_target_pairs={{0,8},{4,12},{8,0},{12,4},{16,24},{20,28},{24,16},{28,20},{1,9},{5... | collective-permute-start | bytes 2457608 | tf_op jit(solution)/shard_map/ppermute | solution.py:742
  28.3 27.8 %collective-permute-start.12 = (bf16[320,1280]{1,0:T(8,128)(2,1)S(1)}, bf16[320,1280]{1,0:T(8,128)(2,1)S(1)}, u32[]{:S(2)}, u32[]{:S(2)}) collective-permute-start(bf16[320,1280]{1,0:T(8,128)(2,1)S(1)} %pad_maximum_fusion.refs_0_.refs_10_), channel_id=1, source_target_pairs={{0,16},{4,20},{8,24},{12,28},{16,0},{20,4},{24,8},{28,12},{1,17},{... | collective-permute-start | bytes 2457608 | tf_op jit(solution)/shard_map/ppermute | solution.py:742
  36.4 19.7 %collective-permute-start.13 = (bf16[320,1280]{1,0:T(8,128)(2,1)S(1)}, bf16[320,1280]{1,0:T(8,128)(2,1)S(1)}, u32[]{:S(2)}, u32[]{:S(2)}) collective-permute-start(bf16[320,1280]{1,0:T(8,128)(2,1)S(1)} %pad_maximum_fusion.refs_0_.refs_10_), channel_id=1, source_target_pairs={{0,4},{4,0},{8,12},{12,8},{16,20},{20,16},{24,28},{28,24},{1,5},{5... | collective-permute-start | bytes 2457608 | tf_op jit(solution)/shard_map/ppermute | solution.py:742
  36.5 17.2 %collective-permute-start.10 = (bf16[256,640]{1,0:T(8,128)(2,1)}, bf16[256,640]{1,0:T(8,128)(2,1)S(1)}, u32[]{:S(2)}, u32[]{:S(2)}) collective-permute-start(bf16[256,640]{1,0:T(8,128)(2,1)} %get-tuple-element.905.c0.refs_10_), channel_id=1, source_target_pairs={{0,1},{1,0},{2,3},{3,2},{4,5},{5,4},{6,7},{7,6},{8,9},{9,8},{10,11... | collective-permute-start | bytes 983048 | tf_op jit(solution)/shard_map/ppermute | solution.py:742
  38.1 18.0 %collective-permute-start.9 = (bf16[256,640]{1,0:T(8,128)(2,1)}, bf16[256,640]{1,0:T(8,128)(2,1)S(1)}, u32[]{:S(2)}, u32[]{:S(2)}) collective-permute-start(bf16[256,640]{1,0:T(8,128)(2,1)} %get-tuple-element.905.c0.refs_10_), channel_id=1, source_target_pairs={{0,2},{1,3},{2,0},{3,1},{4,6},{5,7},{6,4},{7,5},{8,10},{9,11},{10,... | collective-permute-start | bytes 983048 | tf_op jit(solution)/shard_map/ppermute | solution.py:742
  56.2 14.2 %collective-permute-start.17 = (bf16[320,1280]{1,0:T(8,128)(2,1)S(1)}, bf16[320,1280]{1,0:T(8,128)(2,1)S(1)}, u32[]{:S(2)}, u32[]{:S(2)}) collective-permute-start(bf16[320,1280]{1,0:T(8,128)(2,1)S(1)} %collective-permute-done.11.refs_1_.refs_11_), channel_id=1, source_target_pairs={{0,4},{4,0},{8,12},{12,8},{16,20},{20,16},{24,28},{28,24},{1,5},{5... | collective-permute-start | bytes 2457608 | tf_op jit(solution)/shard_map/ppermute | solution.py:742
  56.2 14.1 %collective-permute-start.18 = (bf16[320,1280]{1,0:T(8,128)(2,1)S(1)}, bf16[320,1280]{1,0:T(8,128)(2,1)}, u32[]{:S(2)}, u32[]{:S(2)}) collective-permute-start(bf16[320,1280]{1,0:T(8,128)(2,1)S(1)} %collective-permute-done.12.refs_2_.refs_12_), channel_id=1, source_target_pairs={{0,4},{4,0},{8,12},{12,8},{16,20},{20,16},{24,28},{28,24},{1,5},{5... | collective-permute-start | bytes 2457608 | tf_op jit(solution)/shard_map/ppermute | solution.py:742
  70.4 30.0 %collective-permute-start.23 = (bf16[320,1920]{1,0:T(8,128)(2,1)S(1)}, bf16[320,1920]{1,0:T(8,128)(2,1)}, u32[]{:S(2)}, u32[]{:S(2)}) collective-permute-start(bf16[320,1920]{1,0:T(8,128)(2,1)S(1)} %copy-done.4), channel_id=1, source_target_pairs={{0,8},{4,12},{8,0},{12,4},{16,24},{20,28},{24,16},{28,20},{1,9},{5... | collective-permute-start | bytes 3686408 | tf_op jit(solution)/shard_map/ppermute | solution.py:742
  72.0 30.0 %collective-permute-start.24 = (bf16[320,1920]{1,0:T(8,128)(2,1)S(1)}, bf16[320,1920]{1,0:T(8,128)(2,1)}, u32[]{:S(2)}, u32[]{:S(2)}) collective-permute-start(bf16[320,1920]{1,0:T(8,128)(2,1)S(1)} %copy-done.4), channel_id=1, source_target_pairs={{0,16},{4,20},{8,24},{12,28},{16,0},{20,4},{24,8},{28,12},{1,17},{... | collective-permute-start | bytes 3686408 | tf_op jit(solution)/shard_map/ppermute | solution.py:742
  88.8 13.2 %collective-permute-start.22 = (bf16[64,2560]{1,0:T(8,128)(2,1)}, bf16[64,2560]{1,0:T(8,128)(2,1)S(1)}, u32[]{:S(2)}, u32[]{:S(2)}) collective-permute-start(bf16[64,2560]{1,0:T(8,128)(2,1)} %get-tuple-element.677), channel_id=1, source_target_pairs={{0,1},{1,0},{2,3},{3,2},{4,5},{5,4},{6,7},{7,6},{8,9},{9,8},{10,11... | collective-permute-start | bytes 983048 | tf_op jit(solution)/shard_map/ppermute | solution.py:742
  89.3 36.9 %collective-permute-start.27 = (bf16[320,1920]{1,0:T(8,128)(2,1)S(1)}, bf16[320,1920]{1,0:T(8,128)(2,1)S(1)}, u32[]{:S(2)}, u32[]{:S(2)}) collective-permute-start(bf16[320,1920]{1,0:T(8,128)(2,1)S(1)} %copy-done.5), channel_id=1, source_target_pairs={{0,8},{4,12},{8,0},{12,4},{16,24},{20,28},{24,16},{28,20},{1,9},{5... | collective-permute-start | bytes 3686408 | tf_op jit(solution)/shard_map/ppermute | solution.py:742
  90.2 37.3 %collective-permute-start.28 = (bf16[320,1920]{1,0:T(8,128)(2,1)S(1)}, bf16[320,1920]{1,0:T(8,128)(2,1)}, u32[]{:S(2)}, u32[]{:S(2)}) collective-permute-start(bf16[320,1920]{1,0:T(8,128)(2,1)S(1)} %copy-done.5), channel_id=1, source_target_pairs={{0,16},{4,20},{8,24},{12,28},{16,0},{20,4},{24,8},{28,12},{1,17},{... | collective-permute-start | bytes 3686408 | tf_op jit(solution)/shard_map/ppermute | solution.py:742
  102.0 25.6 %collective-permute-start.29 = (bf16[320,1920]{1,0:T(8,128)(2,1)}, bf16[320,1920]{1,0:T(8,128)(2,1)S(1)}, u32[]{:S(2)}, u32[]{:S(2)}) collective-permute-start(bf16[320,1920]{1,0:T(8,128)(2,1)} %collective-permute-done.23.refs_7_.refs_4_), channel_id=1, source_target_pairs={{0,4},{4,0},{8,12},{12,8},{16,20},{20,16},{24,28},{28,24},{1,5},{5... | collective-permute-start | bytes 3686408 | tf_op jit(solution)/shard_map/ppermute | solution.py:742
  104.7 21.5 %collective-permute-start.26 = (bf16[64,2560]{1,0:T(8,128)(2,1)}, bf16[64,2560]{1,0:T(8,128)(2,1)S(1)}, u32[]{:S(2)}, u32[]{:S(2)}) collective-permute-start(bf16[64,2560]{1,0:T(8,128)(2,1)} %get-tuple-element.685), channel_id=1, source_target_pairs={{0,1},{1,0},{2,3},{3,2},{4,5},{5,4},{6,7},{7,6},{8,9},{9,8},{10,11... | collective-permute-start | bytes 983048 | tf_op jit(solution)/shard_map/ppermute | solution.py:742
  105.1 21.1 %collective-permute-start.25 = (bf16[64,2560]{1,0:T(8,128)(2,1)}, bf16[64,2560]{1,0:T(8,128)(2,1)S(1)}, u32[]{:S(2)}, u32[]{:S(2)}) collective-permute-start(bf16[64,2560]{1,0:T(8,128)(2,1)} %first_add.1), channel_id=1, source_target_pairs={{0,2},{1,3},{2,0},{3,1},{4,6},{5,7},{6,4},{7,5},{8,10},{9,11},{10,... | collective-permute-start | bytes 983048 | tf_op jit(solution)/shard_map/ppermute | solution.py:742
  128.1 29.7 %collective-permute-start.36 = (bf16[320,1920]{1,0:T(8,128)(2,1)}, bf16[320,1920]{1,0:T(8,128)(2,1)}, u32[]{:S(2)}, u32[]{:S(2)}) collective-permute-start(bf16[320,1920]{1,0:T(8,128)(2,1)} %collective-permute-done.24.refs_8_.refs_5_), channel_id=1, source_target_pairs={{0,8},{4,12},{8,0},{12,4},{16,24},{20,28},{24,16},{28,20},{1,9},{5... | collective-permute-start | bytes 3686408 | tf_op jit(solution)/shard_map/ppermute | solution.py:742
  128.7 29.2 %collective-permute-start.37 = (bf16[320,1920]{1,0:T(8,128)(2,1)S(1)}, bf16[320,1920]{1,0:T(8,128)(2,1)}, u32[]{:S(2)}, u32[]{:S(2)}) collective-permute-start(bf16[320,1920]{1,0:T(8,128)(2,1)S(1)} %collective-permute-done.27.refs_15_.refs_12_), channel_id=1, source_target_pairs={{0,16},{4,20},{8,24},{12,28},{16,0},{20,4},{24,8},{28,12},{1,17},{... | collective-permute-start | bytes 3686408 | tf_op jit(solution)/shard_map/ppermute | solution.py:742
  134.3 16.7 %collective-permute-start.34 = (bf16[64,2560]{1,0:T(8,128)(2,1)}, bf16[64,2560]{1,0:T(8,128)(2,1)S(1)}, u32[]{:S(2)}, u32[]{:S(2)}) collective-permute-start(bf16[64,2560]{1,0:T(8,128)(2,1)} %get-tuple-element.721.refs_1_), channel_id=1, source_target_pairs={{0,1},{1,0},{2,3},{3,2},{4,5},{5,4},{6,7},{7,6},{8,9},{9,8},{10,11... | collective-permute-start | bytes 983048 | tf_op jit(solution)/shard_map/ppermute | solution.py:742
  134.7 17.7 %collective-permute-start.33 = (bf16[64,2560]{1,0:T(8,128)(2,1)}, bf16[64,2560]{1,0:T(8,128)(2,1)S(1)}, u32[]{:S(2)}, u32[]{:S(2)}) collective-permute-start(bf16[64,2560]{1,0:T(8,128)(2,1)} %get-tuple-element.721.refs_1_), channel_id=1, source_target_pairs={{0,2},{1,3},{2,0},{3,1},{4,6},{5,7},{6,4},{7,5},{8,10},{9,11},{10,... | collective-permute-start | bytes 983048 | tf_op jit(solution)/shard_map/ppermute | solution.py:742
  160.9 30.4 %collective-permute-start.42 = (bf16[320,1920]{1,0:T(8,128)(2,1)}, bf16[320,1920]{1,0:T(8,128)(2,1)S(1)}, u32[]{:S(2)}, u32[]{:S(2)}) collective-permute-start(bf16[320,1920]{1,0:T(8,128)(2,1)} %shard.5.refs_4_.refs_19_), channel_id=1, source_target_pairs={{0,8},{4,12},{8,0},{12,4},{16,24},{20,28},{24,16},{28,20},{1,9},{5... | collective-permute-start | bytes 3686408 | tf_op jit(solution)/shard_map/ppermute | solution.py:742
  161.4 29.9 %collective-permute-start.43 = (bf16[320,1920]{1,0:T(8,128)(2,1)}, bf16[320,1920]{1,0:T(8,128)(2,1)S(1)}, u32[]{:S(2)}, u32[]{:S(2)}) collective-permute-start(bf16[320,1920]{1,0:T(8,128)(2,1)} %shard.5.refs_4_.refs_19_), channel_id=1, source_target_pairs={{0,16},{4,20},{8,24},{12,28},{16,0},{20,4},{24,8},{28,12},{1,17},{... | collective-permute-start | bytes 3686408 | tf_op jit(solution)/shard_map/ppermute | solution.py:742
  167.9 23.4 %collective-permute-start.41 = (bf16[320,1920]{1,0:T(8,128)(2,1)}, bf16[320,1920]{1,0:T(8,128)(2,1)S(1)}, u32[]{:S(2)}, u32[]{:S(2)}) collective-permute-start(bf16[320,1920]{1,0:T(8,128)(2,1)} %shard.5.refs_4_.refs_19_), channel_id=1, source_target_pairs={{0,4},{4,0},{8,12},{12,8},{16,20},{20,16},{24,28},{28,24},{1,5},{5... | collective-permute-start | bytes 3686408 | tf_op jit(solution)/shard_map/ppermute | solution.py:742
  191.3 12.1 %collective-permute-start.48 = (bf16[1280,1920]{1,0:T(8,128)(2,1)}, bf16[1280,1920]{1,0:T(8,128)(2,1)}, u32[]{:S(2)}, u32[]{:S(2)}) collective-permute-start(bf16[1280,1920]{1,0:T(8,128)(2,1)} %grads_out_ffn_0.1), channel_id=1, source_target_pairs={{0,4},{4,0},{8,12},{12,8},{16,20},{20,16},{24,28},{28,24},{1,5},{5... | collective-permute-start | bytes 14745608 | tf_op jit(solution)/shard_map/ppermute | solution.py:742
  194.2 16.4 %collective-permute-start.45 = (bf16[160,1920]{1,0:T(8,128)(2,1)}, bf16[160,1920]{1,0:T(8,128)(2,1)}, u32[]{:S(2)}, u32[]{:S(2)}) collective-permute-start(bf16[160,1920]{1,0:T(8,128)(2,1)} %slice.35), channel_id=1, source_target_pairs={{0,8},{4,12},{8,0},{12,4},{16,24},{20,28},{24,16},{28,20},{1,9},{5... | collective-permute-start | bytes 1843208 | tf_op jit(solution)/shard_map/ppermute | solution.py:742
  194.8 16.1 %collective-permute-start.44 = (bf16[160,1920]{1,0:T(8,128)(2,1)}, bf16[160,1920]{1,0:T(8,128)(2,1)}, u32[]{:S(2)}, u32[]{:S(2)}) collective-permute-start(bf16[160,1920]{1,0:T(8,128)(2,1)} %slice.34), channel_id=1, source_target_pairs={{0,16},{4,20},{8,24},{12,28},{16,0},{20,4},{24,8},{28,12},{1,17},{... | collective-permute-start | bytes 1843208 | tf_op jit(solution)/shard_map/ppermute | solution.py:742
  214.1 13.2 %collective-permute-start.51 = (bf16[1280,1920]{1,0:T(8,128)(2,1)}, bf16[1280,1920]{1,0:T(8,128)(2,1)}, u32[]{:S(2)}, u32[]{:S(2)}) collective-permute-start(bf16[1280,1920]{1,0:T(8,128)(2,1)} %grads_out_ffn_1.1), channel_id=1, source_target_pairs={{0,4},{4,0},{8,12},{12,8},{16,20},{20,16},{24,28},{28,24},{1,5},{5... | collective-permute-start | bytes 14745608 | tf_op jit(solution)/shard_map/ppermute | solution.py:742
  214.2 29.5 %collective-permute-start.53 = (bf16[320,1920]{1,0:T(8,128)(2,1)}, bf16[320,1920]{1,0:T(8,128)(2,1)S(1)}, u32[]{:S(2)}, u32[]{:S(2)}) collective-permute-start(bf16[320,1920]{1,0:T(8,128)(2,1)} %get-tuple-element.803), channel_id=1, source_target_pairs={{0,8},{4,12},{8,0},{12,4},{16,24},{20,28},{24,16},{28,20},{1,9},{5... | collective-permute-start | bytes 3686408 | tf_op jit(solution)/shard_map/ppermute | solution.py:742
  215.7 29.2 %collective-permute-start.54 = (bf16[320,1920]{1,0:T(8,128)(2,1)}, bf16[320,1920]{1,0:T(8,128)(2,1)S(1)}, u32[]{:S(2)}, u32[]{:S(2)}) collective-permute-start(bf16[320,1920]{1,0:T(8,128)(2,1)} %get-tuple-element.804), channel_id=1, source_target_pairs={{0,16},{4,20},{8,24},{12,28},{16,0},{20,4},{24,8},{28,12},{1,17},{... | collective-permute-start | bytes 3686408 | tf_op jit(solution)/shard_map/ppermute | solution.py:742
  227.3 17.6 %collective-permute-start.52 = (bf16[64,2560]{1,0:T(8,128)(2,1)}, bf16[64,2560]{1,0:T(8,128)(2,1)S(1)}, u32[]{:S(2)}, u32[]{:S(2)}) collective-permute-start(bf16[64,2560]{1,0:T(8,128)(2,1)} %get-tuple-element.800), channel_id=1, source_target_pairs={{0,1},{1,0},{2,3},{3,2},{4,5},{5,4},{6,7},{7,6},{8,9},{9,8},{10,11... | collective-permute-start | bytes 983048 | tf_op jit(solution)/shard_map/ppermute | solution.py:742
  244.9 21.8 %collective-permute-start.57 = (bf16[1280,1920]{1,0:T(8,128)(2,1)}, bf16[1280,1920]{1,0:T(8,128)(2,1)}, u32[]{:S(2)}, u32[]{:S(2)}) collective-permute-start(bf16[1280,1920]{1,0:T(8,128)(2,1)} %grads_out_ffn_2.1), channel_id=1, source_target_pairs={{0,4},{4,0},{8,12},{12,8},{16,20},{20,16},{24,28},{28,24},{1,5},{5... | collective-permute-start | bytes 14745608 | tf_op jit(solution)/shard_map/ppermute | solution.py:742
  246.0 15.9 %collective-permute-start.56 = (bf16[64,2560]{1,0:T(8,128)(2,1)}, bf16[64,2560]{1,0:T(8,128)(2,1)S(1)}, u32[]{:S(2)}, u32[]{:S(2)}) collective-permute-start(bf16[64,2560]{1,0:T(8,128)(2,1)} %get-tuple-element.820), channel_id=1, source_target_pairs={{0,1},{1,0},{2,3},{3,2},{4,5},{5,4},{6,7},{7,6},{8,9},{9,8},{10,11... | collective-permute-start | bytes 983048 | tf_op jit(solution)/shard_map/ppermute | solution.py:742
  247.8 36.0 %collective-permute-start.60 = (bf16[320,1920]{1,0:T(8,128)(2,1)}, bf16[320,1920]{1,0:T(8,128)(2,1)S(1)}, u32[]{:S(2)}, u32[]{:S(2)}) collective-permute-start(bf16[320,1920]{1,0:T(8,128)(2,1)} %get-tuple-element.863), channel_id=1, source_target_pairs={{0,8},{4,12},{8,0},{12,4},{16,24},{20,28},{24,16},{28,20},{1,9},{5... | collective-permute-start | bytes 3686408 | tf_op jit(solution)/shard_map/ppermute | solution.py:742
  248.5 35.4 %collective-permute-start.61 = (bf16[320,1920]{1,0:T(8,128)(2,1)}, bf16[320,1920]{1,0:T(8,128)(2,1)S(1)}, u32[]{:S(2)}, u32[]{:S(2)}) collective-permute-start(bf16[320,1920]{1,0:T(8,128)(2,1)} %get-tuple-element.864), channel_id=1, source_target_pairs={{0,16},{4,20},{8,24},{12,28},{16,0},{20,4},{24,8},{28,12},{1,17},{... | collective-permute-start | bytes 3686408 | tf_op jit(solution)/shard_map/ppermute | solution.py:742
  250.5 16.2 %collective-permute-start.55 = (bf16[64,2560]{1,0:T(8,128)(2,1)S(1)}, bf16[64,2560]{1,0:T(8,128)(2,1)S(1)}, u32[]{:S(2)}, u32[]{:S(2)}) collective-permute-start(bf16[64,2560]{1,0:T(8,128)(2,1)S(1)} %add_convert_fusion.2), channel_id=1, source_target_pairs={{0,2},{1,3},{2,0},{3,1},{4,6},{5,7},{6,4},{7,5},{8,10},{9,11},{10,... | collective-permute-start | bytes 983048 | tf_op jit(solution)/shard_map/ppermute | solution.py:742
  270.8 14.2 %collective-permute-start.59 = (bf16[64,2560]{1,0:T(8,128)(2,1)}, bf16[64,2560]{1,0:T(8,128)(2,1)S(1)}, u32[]{:S(2)}, u32[]{:S(2)}) collective-permute-start(bf16[64,2560]{1,0:T(8,128)(2,1)} %get-tuple-element.891.p0), channel_id=1, source_target_pairs={{0,1},{1,0},{2,3},{3,2},{4,5},{5,4},{6,7},{7,6},{8,9},{9,8},{10,11... | collective-permute-start | bytes 983048 | tf_op jit(solution)/shard_map/ppermute | solution.py:742
  270.8 15.6 %collective-permute-start.58 = (bf16[64,2560]{1,0:T(8,128)(2,1)}, bf16[64,2560]{1,0:T(8,128)(2,1)}, u32[]{:S(2)}, u32[]{:S(2)}) collective-permute-start(bf16[64,2560]{1,0:T(8,128)(2,1)} %get-tuple-element.891.p0), channel_id=1, source_target_pairs={{0,2},{1,3},{2,0},{3,1},{4,6},{5,7},{6,4},{7,5},{8,10},{9,11},{10,... | collective-permute-start | bytes 983048 | tf_op jit(solution)/shard_map/ppermute | solution.py:742
  286.6 45.3 %collective-permute-start.68 = (bf16[480,1920]{1,0:T(8,128)(2,1)}, bf16[480,1920]{1,0:T(8,128)(2,1)S(1)}, u32[]{:S(2)}, u32[]{:S(2)}) collective-permute-start(bf16[480,1920]{1,0:T(8,128)(2,1)} %get-tuple-element.944), channel_id=1, source_target_pairs={{0,8},{4,12},{8,0},{12,4},{16,24},{20,28},{24,16},{28,20},{1,9},{5... | collective-permute-start | bytes 5529608 | tf_op jit(solution)/shard_map/ppermute | solution.py:742
  287.6 44.3 %collective-permute-start.69 = (bf16[480,1920]{1,0:T(8,128)(2,1)}, bf16[480,1920]{1,0:T(8,128)(2,1)}, u32[]{:S(2)}, u32[]{:S(2)}) collective-permute-start(bf16[480,1920]{1,0:T(8,128)(2,1)} %get-tuple-element.945), channel_id=1, source_target_pairs={{0,16},{4,20},{8,24},{12,28},{16,0},{20,4},{24,8},{28,12},{1,17},{... | collective-permute-start | bytes 5529608 | tf_op jit(solution)/shard_map/ppermute | solution.py:742
  294.3 13.9 %collective-permute-start.63 = (bf16[128,2560]{1,0:T(8,128)(2,1)}, bf16[128,2560]{1,0:T(8,128)(2,1)}, u32[]{:S(2)}, u32[]{:S(2)}) collective-permute-start(bf16[128,2560]{1,0:T(8,128)(2,1)} %get-tuple-element.916), channel_id=1, source_target_pairs={{0,1},{1,0},{2,3},{3,2},{4,5},{5,4},{6,7},{7,6},{8,9},{9,8},{10,11... | collective-permute-start | bytes 1966088 | tf_op jit(solution)/shard_map/ppermute | solution.py:742
  316.2 15.7 %collective-permute-start.67 = (bf16[256,640]{1,0:T(8,128)(2,1)}, bf16[256,640]{1,0:T(8,128)(2,1)S(1)}, u32[]{:S(2)}, u32[]{:S(2)}) collective-permute-start(bf16[256,640]{1,0:T(8,128)(2,1)} %get-tuple-element.943), channel_id=1, source_target_pairs={{0,1},{1,0},{2,3},{3,2},{4,5},{5,4},{6,7},{7,6},{8,9},{9,8},{10,11... | collective-permute-start | bytes 983048 | tf_op jit(solution)/shard_map/ppermute | solution.py:742
  318.0 13.9 %collective-permute-start.66 = (bf16[256,640]{1,0:T(8,128)(2,1)S(1)}, bf16[256,640]{1,0:T(8,128)(2,1)}, u32[]{:S(2)}, u32[]{:S(2)}) collective-permute-start(bf16[256,640]{1,0:T(8,128)(2,1)S(1)} %add_convert_fusion.1), channel_id=1, source_target_pairs={{0,2},{1,3},{2,0},{3,1},{4,6},{5,7},{6,4},{7,5},{8,10},{9,11},{10,... | collective-permute-start | bytes 983048 | tf_op jit(solution)/shard_map/ppermute | solution.py:742
  332.0 19.6 %collective-permute-start.70 = (bf16[1280,1280]{1,0:T(8,128)(2,1)}, bf16[1280,1280]{1,0:T(8,128)(2,1)}, u32[]{:S(2)}, u32[]{:S(2)}) collective-permute-start(bf16[1280,1280]{1,0:T(8,128)(2,1)} %grads_out_yo.1), channel_id=1, source_target_pairs={{0,4},{4,0},{8,12},{12,8},{16,20},{20,16},{24,28},{28,24},{1,5},{5... | collective-permute-start | bytes 9830408 | tf_op jit(solution)/shard_map/ppermute | solution.py:742
  332.7 18.9 %collective-permute-start.71 = (bf16[64,2560]{1,0:T(8,128)(2,1)}, bf16[64,2560]{1,0:T(8,128)(2,1)}, u32[]{:S(2)}, u32[]{:S(2)}) collective-permute-start(bf16[64,2560]{1,0:T(8,128)(2,1)} %out_add.1), channel_id=1, source_target_pairs={{0,2},{1,3},{2,0},{3,1},{4,6},{5,7},{6,4},{7,5},{8,10},{9,11},{10,... | collective-permute-start | bytes 983048 | tf_op jit(solution)/shard_map/ppermute | solution.py:742
  334.9 31.4 %collective-permute-start.73 = (bf16[160,1920]{1,0:T(8,128)(2,1)}, bf16[160,1920]{1,0:T(8,128)(2,1)S(1)}, u32[]{:S(2)}, u32[]{:S(2)}) collective-permute-start(bf16[160,1920]{1,0:T(8,128)(2,1)} %get-tuple-element.1007), channel_id=1, source_target_pairs={{0,8},{4,12},{8,0},{12,4},{16,24},{20,28},{24,16},{28,20},{1,9},{5... | collective-permute-start | bytes 1843208 | tf_op jit(solution)/shard_map/ppermute | solution.py:742
  335.7 30.5 %collective-permute-start.74 = (bf16[160,1920]{1,0:T(8,128)(2,1)}, bf16[160,1920]{1,0:T(8,128)(2,1)}, u32[]{:S(2)}, u32[]{:S(2)}) collective-permute-start(bf16[160,1920]{1,0:T(8,128)(2,1)} %get-tuple-element.1008), channel_id=1, source_target_pairs={{0,16},{4,20},{8,24},{12,28},{16,0},{20,4},{24,8},{28,12},{1,17},{... | collective-permute-start | bytes 1843208 | tf_op jit(solution)/shard_map/ppermute | solution.py:742
  337.9 28.3 %collective-permute-start.75 = (bf16[5,4,64,128]{3,2,1,0:T(8,128)(2,1)S(1)}, bf16[5,4,64,128]{3,2,1,0:T(8,128)(2,1)}, u32[]{:S(2)}, u32[]{:S(2)}) collective-permute-start(bf16[5,4,64,128]{3,2,1,0:T(8,128)(2,1)S(1)} %copy-done.44), channel_id=1, source_target_pairs={{0,8},{4,12},{8,0},{12,4},{16,24},{20,28},{24,16},{28,20},{1,9},{5... | collective-permute-start | bytes 983048 | tf_op jit(solution)/shard_map/ppermute | solution.py:742
  351.6 14.7 %collective-permute-start.72 = (bf16[64,2560]{1,0:T(8,128)(2,1)}, bf16[64,2560]{1,0:T(8,128)(2,1)S(1)}, u32[]{:S(2)}, u32[]{:S(2)}) collective-permute-start(bf16[64,2560]{1,0:T(8,128)(2,1)} %get-tuple-element.993), channel_id=1, source_target_pairs={{0,1},{1,0},{2,3},{3,2},{4,5},{5,4},{6,7},{7,6},{8,9},{9,8},{10,11... | collective-permute-start | bytes 983048 | tf_op jit(solution)/shard_map/ppermute | solution.py:742
  366.3 21.9 %collective-permute-start.78 = (bf16[1280,640]{1,0:T(8,128)(2,1)}, bf16[1280,640]{1,0:T(8,128)(2,1)S(1)}, u32[]{:S(2)}, u32[]{:S(2)}) collective-permute-start(bf16[1280,640]{1,0:T(8,128)(2,1)} %grads_out_x.1), channel_id=1, source_target_pairs={{0,4},{4,0},{8,12},{12,8},{16,20},{20,16},{24,28},{28,24},{1,5},{5... | collective-permute-start | bytes 4915208 | tf_op jit(solution)/shard_map/ppermute | solution.py:742
  367.1 20.1 %collective-permute-start.79 = (bf16[320,1280]{1,0:T(8,128)(2,1)}, bf16[320,1280]{1,0:T(8,128)(2,1)S(1)}, u32[]{:S(2)}, u32[]{:S(2)}) collective-permute-start(bf16[320,1280]{1,0:T(8,128)(2,1)} %get-tuple-element.1025), channel_id=1, source_target_pairs={{0,8},{4,12},{8,0},{12,4},{16,24},{20,28},{24,16},{28,20},{1,9},{5... | collective-permute-start | bytes 2457608 | tf_op jit(solution)/shard_map/ppermute | solution.py:742
  368.3 19.9 %collective-permute-start.80 = (bf16[320,1280]{1,0:T(8,128)(2,1)}, bf16[320,1280]{1,0:T(8,128)(2,1)S(1)}, u32[]{:S(2)}, u32[]{:S(2)}) collective-permute-start(bf16[320,1280]{1,0:T(8,128)(2,1)} %get-tuple-element.1026), channel_id=1, source_target_pairs={{0,16},{4,20},{8,24},{12,28},{16,0},{20,4},{24,8},{28,12},{1,17},{... | collective-permute-start | bytes 2457608 | tf_op jit(solution)/shard_map/ppermute | solution.py:742
  369.5 16.2 %collective-permute-start.77 = (bf16[64,2560]{1,0:T(8,128)(2,1)S(1)}, bf16[64,2560]{1,0:T(8,128)(2,1)S(1)}, u32[]{:S(2)}, u32[]{:S(2)}) collective-permute-start(bf16[64,2560]{1,0:T(8,128)(2,1)S(1)} %copy-done.84), channel_id=1, source_target_pairs={{0,1},{1,0},{2,3},{3,2},{4,5},{5,4},{6,7},{7,6},{8,9},{9,8},{10,11... | collective-permute-start | bytes 983048 | tf_op jit(solution)/shard_map/ppermute | solution.py:742
  369.6 16.1 %collective-permute-start.76 = (bf16[64,2560]{1,0:T(8,128)(2,1)S(1)}, bf16[64,2560]{1,0:T(8,128)(2,1)S(1)}, u32[]{:S(2)}, u32[]{:S(2)}) collective-permute-start(bf16[64,2560]{1,0:T(8,128)(2,1)S(1)} %add_convert_fusion), channel_id=1, source_target_pairs={{0,2},{1,3},{2,0},{3,1},{4,6},{5,7},{6,4},{7,5},{8,10},{9,11},{10,... | collective-permute-start | bytes 983048 | tf_op jit(solution)/shard_map/ppermute | solution.py:742
  392.4 18.3 %collective-permute-start.83 = (bf16[160,1920]{1,0:T(8,128)(2,1)}, bf16[160,1920]{1,0:T(8,128)(2,1)}, u32[]{:S(2)}, u32[]{:S(2)}) collective-permute-start(bf16[160,1920]{1,0:T(8,128)(2,1)} %get-tuple-element.1044), channel_id=1, source_target_pairs={{0,8},{4,12},{8,0},{12,4},{16,24},{20,28},{24,16},{28,20},{1,9},{5... | collective-permute-start | bytes 1843208 | tf_op jit(solution)/shard_map/ppermute | solution.py:742
  393.2 17.5 %collective-permute-start.84 = (bf16[160,1920]{1,0:T(8,128)(2,1)}, bf16[160,1920]{1,0:T(8,128)(2,1)S(1)}, u32[]{:S(2)}, u32[]{:S(2)}) collective-permute-start(bf16[160,1920]{1,0:T(8,128)(2,1)} %get-tuple-element.1045), channel_id=1, source_target_pairs={{0,16},{4,20},{8,24},{12,28},{16,0},{20,4},{24,8},{28,12},{1,17},{... | collective-permute-start | bytes 1843208 | tf_op jit(solution)/shard_map/ppermute | solution.py:742
  393.5 17.2 %collective-permute-start.82 = (bf16[64,2560]{1,0:T(8,128)(2,1)}, bf16[64,2560]{1,0:T(8,128)(2,1)S(1)}, u32[]{:S(2)}, u32[]{:S(2)}) collective-permute-start(bf16[64,2560]{1,0:T(8,128)(2,1)} %first_back.1.refs_0_), channel_id=1, source_target_pairs={{0,1},{1,0},{2,3},{3,2},{4,5},{5,4},{6,7},{7,6},{8,9},{9,8},{10,11... | collective-permute-start | bytes 983048 | tf_op jit(solution)/shard_map/ppermute | solution.py:742
  394.5 16.2 %collective-permute-start.81 = (bf16[64,2560]{1,0:T(8,128)(2,1)}, bf16[64,2560]{1,0:T(8,128)(2,1)S(1)}, u32[]{:S(2)}, u32[]{:S(2)}) collective-permute-start(bf16[64,2560]{1,0:T(8,128)(2,1)} %first_back.1.refs_0_), channel_id=1, source_target_pairs={{0,2},{1,3},{2,0},{3,1},{4,6},{5,7},{6,4},{7,5},{8,10},{9,11},{10,... | collective-permute-start | bytes 983048 | tf_op jit(solution)/shard_map/ppermute | solution.py:742
  397.2 13.5 %collective-permute-start.85 = (f32[2,2560]{1,0:T(2,128)S(1)}, f32[2,2560]{1,0:T(2,128)S(1)}, u32[]{:S(2)}, u32[]{:S(2)}) collective-permute-start(f32[2,2560]{1,0:T(2,128)S(1)} %pad_maximum_fusion.2), channel_id=1, source_target_pairs={{0,1},{1,0},{2,3},{3,2},{4,5},{5,4},{6,7},{7,6},{8,9},{9,8},{10,11... | collective-permute-start | bytes 61448 | tf_op jit(solution)/shard_map/ppermute | solution.py:742
  410.8 17.6 %collective-permute-start.88 = (bf16[640,640]{1,0:T(8,128)(2,1)}, bf16[640,640]{1,0:T(8,128)(2,1)S(1)}, u32[]{:S(2)}, u32[]{:S(2)}) collective-permute-start(bf16[640,640]{1,0:T(8,128)(2,1)} %get-tuple-element.1074), channel_id=1, source_target_pairs={{0,8},{4,12},{8,0},{12,4},{16,24},{20,28},{24,16},{28,20},{1,9},{5... | collective-permute-start | bytes 2457608 | tf_op jit(solution)/shard_map/ppermute | solution.py:742
  411.4 18.2 %collective-permute-start.89 = (bf16[640,640]{1,0:T(8,128)(2,1)}, bf16[640,640]{1,0:T(8,128)(2,1)S(1)}, u32[]{:S(2)}, u32[]{:S(2)}) collective-permute-start(bf16[640,640]{1,0:T(8,128)(2,1)} %get-tuple-element.1075), channel_id=1, source_target_pairs={{0,16},{4,20},{8,24},{12,28},{16,0},{20,4},{24,8},{28,12},{1,17},{... | collective-permute-start | bytes 2457608 | tf_op jit(solution)/shard_map/ppermute | solution.py:742
  412.4 15.5 %collective-permute-start.90 = (bf16[64,2560]{1,0:T(8,128)(2,1)}, bf16[64,2560]{1,0:T(8,128)(2,1)S(1)}, u32[]{:S(2)}, u32[]{:S(2)}) collective-permute-start(bf16[64,2560]{1,0:T(8,128)(2,1)} %block_out.1.refs_5_), channel_id=1, source_target_pairs={{0,2},{1,3},{2,0},{3,1},{4,6},{5,7},{6,4},{7,5},{8,10},{9,11},{10,... | collective-permute-start | bytes 983048 | tf_op jit(solution)/shard_map/ppermute | solution.py:742
  413.7 14.3 %collective-permute-start.86 = (bf16[64,2560]{1,0:T(8,128)(2,1)S(1)}, bf16[64,2560]{1,0:T(8,128)(2,1)}, u32[]{:S(2)}, u32[]{:S(2)}) collective-permute-start(bf16[64,2560]{1,0:T(8,128)(2,1)S(1)} %collective-permute-done.81.refs_2_), channel_id=1, source_target_pairs={{0,1},{1,0},{2,3},{3,2},{4,5},{5,4},{6,7},{7,6},{8,9},{9,8},{10,11... | collective-permute-start | bytes 983048 | tf_op jit(solution)/shard_map/ppermute | solution.py:742
  415.4 12.5 %collective-permute-start.87 = (f32[2,2560]{1,0:T(2,128)S(1)}, f32[2,2560]{1,0:T(2,128)S(1)}, u32[]{:S(2)}, u32[]{:S(2)}) collective-permute-start(f32[2,2560]{1,0:T(2,128)S(1)} %add.25), channel_id=1, source_target_pairs={{0,2},{1,3},{2,0},{3,1},{4,6},{5,7},{6,4},{7,5},{8,10},{9,11},{10,... | collective-permute-start | bytes 61448 | tf_op jit(solution)/shard_map/ppermute | solution.py:742
  430.5 14.6 %collective-permute-start.93 = (bf16[128,2560]{1,0:T(8,128)(2,1)}, bf16[128,2560]{1,0:T(8,128)(2,1)S(1)}, u32[]{:S(2)}, u32[]{:S(2)}) collective-permute-start(bf16[128,2560]{1,0:T(8,128)(2,1)} %pad_maximum_fusion.1), channel_id=1, source_target_pairs={{0,1},{1,0},{2,3},{3,2},{4,5},{5,4},{6,7},{7,6},{8,9},{9,8},{10,11... | collective-permute-start | bytes 1966088 | tf_op jit(solution)/shard_map/ppermute | solution.py:742
  (121 other events, 805.9 us)
where the time goes:
time: 468 us; the launch traced here: 460 us
  Pallas kernels  209 us (45%)
  waiting for transfers between devices  135 us (29%)
  starting transfers between devices  88.3 us (19%)
  local copies, waits for them, and re-layouts  22.3 us (5%)
    pallas_call x39, Pallas kernels, call(): pl.pallas_call(kernel, grid=(1,), out_shape=outs, in_specs=[smem] * scala...  180 us
    ppermute x100, waiting for transfers between devices, exchange(): return lax.ppermute(v, axis, [(i, i ^ bit) for i in range(size)])  135 us
    ppermute x100, starting transfers between devices, exchange(): return lax.ppermute(v, axis, [(i, i ^ bit) for i in range(size)])  88.3 us
    pallas_call x1, Pallas kernels, body(): pl.pallas_call(partial(backward_scan_kernel, len(all_yo)), in_specs=[smem...  11.1 us
    pallas_call x1, Pallas kernels, body(): pl.pallas_call(partial(conv_back_kernel, size, len(all_x)), in_specs=[sme...  10.7 us
    unnamed x173, local copies, waits for them, and re-layouts  10.5 us
  transfers between devices with their start and end apart: 100, of which 42 were waited for; matrix products, arithmetic and copies ran while one was open for 3% of the time, Pallas kernels for 43%

commit v1 on v0

--- a/solution.py
+++ b/solution.py
@@ -474,7 +474,12 @@
         return copy
 
     held = []
-    if not first:
+    if first:
+        for k, piece in enumerate(pieces):
+            count = piece.shape[0]
+            at = pl.multiple_of((z_ref[0] ^ k) * count, count)
+            held.append(load(piece, s_ref.at[pl.ds(at, count)]))
+    else:
         held.append(load(s_any, s_ref))
     held.append(load(cot_any, cot_ref))
     landing = []
@@ -486,8 +491,6 @@
         landing.append(marks)
     if not first:
         sums = load(in_grad, acc_grad)
-    if first:
-        assemble_kernel(z_ref, *pieces, s_ref)
     for copy in held:
         copy.wait()
     stores = []
@@ -679,8 +682,8 @@
     out_ref[...] = (a_ref[...].astype(f32) + b_ref[...].astype(f32)).astype(out_ref.dtype)
 
 
-def small_kernel(units, sums_ref, by_x, by_y, across, taps_ref, bias_ref, rate_ref, input_ref, decay_ref, one_ref, two_ref):
-    total = (sums_ref[...] + by_x[...]) + (by_y[...] + across[...])
+def small_kernel(units, sums_ref, by_y, taps_ref, bias_ref, rate_ref, input_ref, decay_ref, one_ref, two_ref):
+    total = sums_ref[...] + by_y[...]
     heads, taps, _ = taps_ref.shape
     for h in range(heads):
         cols = slice(h * units, (h + 1) * units)
@@ -696,20 +699,24 @@
 
 
 def last_kernel(units, z_ref, *refs):
-    x_ins, block_ins, gate_ins, small_ins = refs[:5], refs[5:9], refs[9:11], refs[11:15]
-    x_ref, block_ref, rate_ref, input_ref = refs[15:19]
+    x_ins, block_ins, gate_ins, small_ins, tok_ins = (
+        refs[:5], refs[5:9], refs[9:13], refs[13:15], refs[15:19]
+    )
+    x_ref, block_ref, tok_ref, rate_ref, input_ref = refs[19:24]
     join_x_kernel(*x_ins, x_ref)
     assemble_kernel(z_ref, *block_ins, block_ref)
+    assemble_kernel(z_ref, *tok_ins, tok_ref)
     gate_join_kernel(z_ref, *gate_ins, rate_ref, input_ref)
-    small_kernel(units, *small_ins, *refs[19:])
-
-
-def gate_join_kernel(z_ref, mine_ref, other_ref, rate_ref, input_ref):
+    small_kernel(units, *small_ins, *refs[24:])
+
+
+def gate_join_kernel(z_ref, mine_ref, mine_got, other_ref, other_got, rate_ref, input_ref):
     pairs, _, units, _ = mine_ref.shape
     core = z_ref[1] % 2
-    for src, head in ((mine_ref, core), (other_ref, 1 - core)):
+    for src, got, head in ((mine_ref, mine_got, core), (other_ref, other_got, 1 - core)):
         for p in range(pairs):
-            whole = jnp.concatenate([src[p, z_ref[0] ^ owner] for owner in range(4)], axis=0)
+            parts = [(src[p, z_ref[0] ^ k], got[p, z_ref[0] ^ k]) for k in range(4)]
+            whole = jnp.concatenate([a.astype(f32) + b.astype(f32) for a, b in parts], axis=0)
             rate_ref[2 * p + head] = whole[:, :units].T
             input_ref[2 * p + head] = whole[:, units:].T
 
@@ -1086,11 +1093,11 @@
             pltpu.VMEM((count, width), f32),
             pltpu.VMEM((len(groups), model, 3 * width), bf16),
             pltpu.VMEM((count, model), f32),
-            pltpu.SemaphoreType.DMA((len(weights) + 3,)),
+            pltpu.SemaphoreType.DMA((len(weights) + 6,)),
             pltpu.SemaphoreType.DMA((5,)),
         ]
         ins = [ids, *left, *sums, cot_rel, *weights]
-        at = 1 + len(left) * first
+        at = 1
         return run(
             partial(ffn_kernel, len(groups), first, last), outs, *ins, scalars=1, scratch=scratch,
             specs={i: anywhere for i in range(at, len(ins))}, out_specs=out_specs, name=name,
@@ -1275,7 +1282,7 @@
         ]
     tok3, gains, slot3, block2 = wait(tok3, gains, slot3, block2)
     small = jnp.concatenate([scan_sums, conv_sums, gains.reshape(8, chan)], axis=0)
-    small = sum_over(small, "dp", size, 1, 2)
+    small = sum_over(small, "dp", size, 1, 4)
     block13 = neighbour(jnp.concatenate([block_rows, block2], axis=0))
     gate_got = along(size, 4, after(gate_sum))
     x_last = move(size, *relay(run, [sx_cut], slot3, 2, [], "relay_4"))
@@ -1287,27 +1294,25 @@
         y_share, out_share = run(
             join_yo_kernel, [like((chan, part), f32)] * 2, *yo_ins, specs=specs, name="join_yo"
         )
-    tokens_grad = assemble([tokens_rows, tok1, tok2, tok3], f32, "tokens_grad_all")
-    (gate_sum,) = run(
-        add_kernel, [like(gate_half.shape, f32)], gate_sum, wait(gate_got), name="gate_add"
-    )
-    x_last, block13, small, gate_sum = wait(x_last, block13, small, gate_sum)
+    x_last, block13, small, gate_got = wait(x_last, block13, small, gate_got)
     block_ins = [block_rows, block13, block2, block13]
     block_specs = {2: block((rows, model), 0, 0), 4: block((rows, model), 1, 0)}
     if size == 8:
-        by_x, by_y, across = [exchange(small, "dp", size, bit) for bit in (2, 4, 6)]
-        gate_got = sibling(gate_sum)
-        gate_got, by_x, by_y, across = wait(gate_got, by_x, by_y, across)
-        ins = [ids, sx_cut[0], *slot3, *x_last, *block_ins, gate_sum, gate_got, small, by_x, by_y, across]
+        by_y = exchange(small, "dp", size, 4)
+        gate_other, got_other = sibling(gate_sum), sibling(gate_got)
+        gate_other, got_other, by_y = wait(gate_other, got_other, by_y)
+        ins = [ids, sx_cut[0], *slot3, *x_last, *block_ins, gate_sum, gate_got, gate_other, got_other]
+        ins += [small, by_y, tokens_rows, tok1, tok2, tok3]
         specs = {k: block((q, chan), 3 if k < 4 else 0, 0) for k in range(2, 6)}
         specs.update({6 + k: v for k, v in ((1, block_specs[2]), (3, block_specs[4]))})
         head_like, gate_like = like((heads, units), f32), like((heads, units, 4 * units), f32)
         (
-            x_share, block_out, rate_grad, input_grad, taps_grad, bias_grad, rate_b_grad,
+            x_share, block_out, tokens_grad, rate_grad, input_grad, taps_grad, bias_grad, rate_b_grad,
             input_b_grad, decay_grad, one_grad, two_grad,
         ) = run(
             partial(last_kernel, units),
-            [like((chan, part), f32), like((count, model), bf16), gate_like, gate_like]
+            [like((chan, part), f32), like((count, model), bf16), like((count, model), f32)]
+            + [gate_like, gate_like]
             + [like((heads, taps, units), f32)] + [head_like] * 4 + [like((model,), f32)] * 2,
             *ins, scalars=1, specs=specs, name="last",
         )
@@ -1315,7 +1320,8 @@
         taps_grad = taps_grad.transpose(1, 0, 2)
     else:
         block_out = assemble(block_ins, bf16, "block_out_all", block_specs)
-        small = sum_over(small, "dp", size, 2)
+        tokens_grad = assemble([tokens_rows, tok1, tok2, tok3], f32, "tokens_grad_all")
+        small = sum_over(small, "dp", size, 4)
         taps_grad = small[8 : 8 + taps].reshape(taps, heads, units)
         bias_grad, rate_b_grad, input_b_grad, decay_grad = [
             small[k].reshape(heads, units) for k in (8 + taps, 1, 2, 0)

time: 468 us -> 466 us (level)
  waiting for transfers between devices: 135 us -> 140 us
    ppermute x100, waiting for transfers between devices: 135 us -> 140 us  [exchange(): return lax.ppermute(v, axis, [(i, i ^ bit) for i in range(size)])]
    pallas_call x39 -> x37, Pallas kernels: 180 us -> 177 us  [call(): pl.pallas_call(kernel, grid=(1,), out_shape=outs, in_specs=[smem] * scala...]
    unnamed x173 -> x171, local copies, waits for them, and re-layouts: 10.5 us -> 9.58 us
  transfers between devices with their start and end apart: 100 -> 100, of which waited for: 42 -> 45; matrix products, arithmetic and copies ran while one was open for 3% -> 3% of each run, Pallas kernels for 43% -> 42%
where the time goes in v1:
time: 466 us; the launch traced here: 458 us
  Pallas kernels  205 us (44%)
  waiting for transfers between devices  140 us (30%)
  starting transfers between devices  85.3 us (18%)
  local copies, waits for them, and re-layouts  21.4 us (5%)
    pallas_call x37, Pallas kernels, call(): pl.pallas_call(kernel, grid=(1,), out_shape=outs, in_specs=[smem] * scala...  177 us
    ppermute x100, waiting for transfers between devices, exchange(): return lax.ppermute(v, axis, [(i, i ^ bit) for i in range(size)])  140 us
    ppermute x100, starting transfers between devices, exchange(): return lax.ppermute(v, axis, [(i, i ^ bit) for i in range(size)])  85.3 us
    pallas_call x1, Pallas kernels, body(): pl.pallas_call(partial(backward_scan_kernel, len(all_yo)), in_specs=[smem...  11.1 us
    pallas_call x1, Pallas kernels, body(): pl.pallas_call(partial(conv_back_kernel, size, len(all_x)), in_specs=[sme...  10.7 us
    unnamed x171, local copies, waits for them, and re-layouts  9.58 us
  transfers between devices with their start and end apart: 100, of which 45 were waited for; matrix products, arithmetic and copies ran while one was open for 3% of the time, Pallas kernels for 42%

profile of v1, /device:TPU:0, one launch (start us, length us, event | category | flops | bytes accessed | tf_op | source)
XLA Modules:
  0.0 458.0 jit_solution(15143018722174204986)
XLA Ops:
  2.4 2.6 collective-permute-start.1
  6.5 2.4 shard.3.refs_6_.refs_3_
  12.9 2.2 collective-permute-done.1.refs_2_
  19.8 4.1 norm_first.1
  30.8 5.6 %branch.1 = (f32[256,640]{1,0:T(8,128)}, bf16[256,640]{1,0:T(8,128)(2,1)}) custom-call(bf16[256,2560]{1,0:T(8,128)(2,1)} %get-tuple-element.1034.nf_ref.refs_0_, f32[4,640]{1,0:T(4,128)} %reshape.98.taps_ref, f32[1,640]{1,0:T(1,128)} %reshape.99.bias_ref, f32[3,256,128]{2,1,0:T(8,128)} %broadcast_in_dim.2.mask_ref.refs_17_, bf16[320,640]{1,0:T(8,128)(2,1)} %copy.47.refs_0_, ...), custom_call_target="tpu_custom_call" | custom-call | flops 1 | bytes 1 | tf_op jit(solution)/shard_map/branch/pallas_call | solution.py:51
  38.2 2.6 collective-permute-start.9
  40.8 2.5 shard.4.refs_14_.refs_11_
  43.2 2.7 gate_blocks.1.block_ref.refs_14_
  46.0 7.8 %collective-permute-done.10.c1.refs_11_ = bf16[256,640]{1,0:T(8,128)(2,1)S(1)} collective-permute-done((bf16[256,640]{1,0:T(8,128)(2,1)}, bf16[256,640]{1,0:T(8,128)(2,1)S(1)}, u32[]{:S(2)}, u32[]{:S(2)}) %collective-permute-start.10) | collective-permute-done | bytes 327712 | tf_op jit(solution)/shard_map/ppermute | solution.py:749
  53.8 2.4 collective-permute-done.9.c2.refs_12_
  60.5 3.4 cotangent.1.refs_5_.refs_1_.refs_3_.cot_ref
  63.9 5.2 %collective-permute-done.14.c3.refs_13_ = bf16[256,640]{1,0:T(8,128)(2,1)S(1)} collective-permute-done((bf16[256,640]{1,0:T(8,128)(2,1)}, bf16[256,640]{1,0:T(8,128)(2,1)S(1)}, u32[]{:S(2)}, u32[]{:S(2)}) %collective-permute-start.14) | collective-permute-done | bytes 327712 | tf_op jit(solution)/shard_map/ppermute | solution.py:749
  73.1 6.5 %forward_scan.1 = (f32[256,640]{1,0:T(8,128)}, f32[256,640]{1,0:T(8,128)}, f32[256,640]{1,0:T(8,128)}) custom-call(bf16[256,640]{1,0:T(8,128)(2,1)} %get-tuple-element.901.c0.refs_10_, bf16[256,640]{1,0:T(8,128)(2,1)} %copy-done.41, bf16[256,640]{1,0:T(8,128)(2,1)} %copy-done.42, bf16[256,640]{1,0:T(8,128)(2,1)} %copy-done.43, ...), custom_call_target="tpu_custom_call" | custom-call | flops 1 | bytes 1 | tf_op jit(solution)/shard_map/forward_scan/pallas_call | solution.py:1031
  80.5 8.3 %mix.1 = (f32[256,640]{1,0:T(8,128)}, bf16[256,640]{1,0:T(8,128)(2,1)}, f32[64,2560]{1,0:T(8,128)}, bf16[64,2560]{1,0:T(8,128)(2,1)}, f32[64,2560]{1,0:T(8,128)}, /*index=5*/bf16[64,2560]{1,0:T(8,128)(2,1)}) custom-call(s32[2]{0:T(128)} %pad_add_fusion.z_ref.refs_0_, bf16[256,2560]{1,0:T(8,128)(2,1)} %get-tuple-element.1034.nf_ref.refs_0_, ...), custom_call_target="tpu_custom_call" | custom-call | flops 1 | bytes 1 | tf_op jit(solution)/shard_map/mix/pallas_call | solution.py:51
  91.3 9.2 %collective-permute-done.23.refs_7_.refs_4_ = bf16[320,1920]{1,0:T(8,128)(2,1)} collective-permute-done((bf16[320,1920]{1,0:T(8,128)(2,1)S(1)}, bf16[320,1920]{1,0:T(8,128)(2,1)}, u32[]{:S(2)}, u32[]{:S(2)}) %collective-permute-start.23) | collective-permute-done | bytes 1228832 | tf_op jit(solution)/shard_map/ppermute | solution.py:749
  105.1 2.6 collective-permute-start.25
  107.7 18.5 %collective-permute-done.27.refs_15_.refs_12_ = bf16[320,1920]{1,0:T(8,128)(2,1)S(1)} collective-permute-done((bf16[320,1920]{1,0:T(8,128)(2,1)S(1)}, bf16[320,1920]{1,0:T(8,128)(2,1)S(1)}, u32[]{:S(2)}, u32[]{:S(2)}) %collective-permute-start.27) | collective-permute-done | bytes 1228832 | tf_op jit(solution)/shard_map/ppermute | solution.py:749
  129.6 2.8 norm_second.1
  134.8 2.6 collective-permute-start.33
  137.4 2.4 shard.5.refs_4_.refs_19_
  139.7 11.3 %collective-permute-done.34.refs_2_ = bf16[64,2560]{1,0:T(8,128)(2,1)S(1)} collective-permute-done((bf16[64,2560]{1,0:T(8,128)(2,1)}, bf16[64,2560]{1,0:T(8,128)(2,1)S(1)}, u32[]{:S(2)}, u32[]{:S(2)}) %collective-permute-start.34) | collective-permute-done | bytes 327712 | tf_op jit(solution)/shard_map/ppermute | solution.py:749
  152.7 5.1 %collective-permute-done.36.refs_9_.refs_6_ = bf16[320,1920]{1,0:T(8,128)(2,1)} collective-permute-done((bf16[320,1920]{1,0:T(8,128)(2,1)}, bf16[320,1920]{1,0:T(8,128)(2,1)}, u32[]{:S(2)}, u32[]{:S(2)}) %collective-permute-start.36) | collective-permute-done | bytes 1228832 | tf_op jit(solution)/shard_map/ppermute | solution.py:749
  157.9 2.3 collective-permute-done.35.refs_4_
  162.4 2.4 collective-permute-done.40.refs_18_.refs_15_
  168.1 18.4 %ffn_01.1 = (bf16[256,1280]{1,0:T(8,128)(2,1)}, bf16[256,640]{1,0:T(8,128)(2,1)}, bf16[256,1280]{1,0:T(8,128)(2,1)}, bf16[256,640]{1,0:T(8,128)(2,1)}, bf16[256,2560]{1,0:T(8,128)(2,1)}, /*index=5*/f32[256,2560]{1,0:T(8,128)}) custom-call(s32[2]{0:T(128)} %pad_add_fusion.z_ref.refs_0_, bf16[64,2560]{1,0:T(8,128)(2,1)} %get-tuple-element.717.refs_1_, ...), custom_call_target="tpu_custom_call" | custom-call | flops 1 | bytes 1 | tf_op jit(solution)/shard_map/ffn_01/pallas_call | solution.py:51
  186.5 4.6 %grads_out_ffn_0.1 = bf16[1280,1920]{1,0:T(8,128)(2,1)} custom-call(bf16[256,2560]{1,0:T(8,128)(2,1)} %get-tuple-element.867.refs_0_.refs_1_, bf16[256,2560]{1,0:T(8,128)(2,1)} %cotangent.1.refs_5_.refs_1_.refs_3_.cot_ref, bf16[256,1280]{1,0:T(8,128)(2,1)} %get-tuple-element.762.refs_2_, bf16[256,640]{1,0:T(8,128)(2,1)} %get-tuple-element.819.refs_3_.refs_0_), custom_call_target="tpu_custom_call" | custom-call | flops 1 | bytes 1 | tf_op jit(solution)/shard_map/grads_out_ffn_0/pallas_call | solution.py:51
  195.6 4.6 %grads_out_ffn_1.1 = bf16[1280,1920]{1,0:T(8,128)(2,1)} custom-call(bf16[256,2560]{1,0:T(8,128)(2,1)} %get-tuple-element.867.refs_0_.refs_1_, bf16[256,2560]{1,0:T(8,128)(2,1)} %cotangent.1.refs_5_.refs_1_.refs_3_.cot_ref, bf16[256,1280]{1,0:T(8,128)(2,1)} %get-tuple-element.805.refs_2_, bf16[256,640]{1,0:T(8,128)(2,1)} %get-tuple-element.820.refs_3_.refs_1_), custom_call_target="tpu_custom_call" | custom-call | flops 1 | bytes 1 | tf_op jit(solution)/shard_map/grads_out_ffn_1/pallas_call | solution.py:51
  200.2 2.9 collective-permute-done.47.refs_11_.refs_26_
  203.3 7.2 %grads_own_ffn_0.1 = (f32[320,1920]{1,0:T(8,128)}, f32[160,1920]{1,0:T(8,128)}, f32[160,1920]{1,0:T(8,128)}, bf16[320,1920]{1,0:T(8,128)(2,1)}, bf16[320,1920]{1,0:T(8,128)(2,1)}) custom-call(bf16[256,2560]{1,0:T(8,128)(2,1)} %get-tuple-element.867.refs_0_.refs_1_, bf16[256,2560]{1,0:T(8,128)(2,1)} %cotangent.1.refs_5_.refs_1_.refs_3_.cot_ref, ...), custom_call_target="tpu_custom_call" | custom-call | flops 1 | bytes 1 | tf_op jit(solution)/shard_map/grads_own_ffn_0/pallas_call | solution.py:51
  216.1 11.1 %ffn_2.1 = (bf16[256,1280]{1,0:T(8,128)(2,1)}, bf16[256,640]{1,0:T(8,128)(2,1)}, f32[64,2560]{1,0:T(8,128)}, bf16[64,2560]{1,0:T(8,128)(2,1)}, f32[64,2560]{1,0:T(8,128)}, /*index=5*/bf16[64,2560]{1,0:T(8,128)(2,1)}) custom-call(s32[2]{0:T(128)} %pad_add_fusion.z_ref.refs_0_, bf16[256,2560]{1,0:T(8,128)(2,1)} %get-tuple-element.867.refs_0_.refs_1_, ...), custom_call_target="tpu_custom_call" | custom-call | flops 1 | bytes 1 | tf_op jit(solution)/shard_map/ffn_2/pallas_call | solution.py:51
  228.7 7.2 %grads_own_ffn_1.1 = (f32[320,1920]{1,0:T(8,128)}, f32[160,1920]{1,0:T(8,128)}, f32[160,1920]{1,0:T(8,128)}, bf16[320,1920]{1,0:T(8,128)(2,1)}, bf16[320,1920]{1,0:T(8,128)(2,1)}) custom-call(bf16[256,2560]{1,0:T(8,128)(2,1)} %get-tuple-element.867.refs_0_.refs_1_, bf16[256,2560]{1,0:T(8,128)(2,1)} %cotangent.1.refs_5_.refs_1_.refs_3_.cot_ref, ...), custom_call_target="tpu_custom_call" | custom-call | flops 1 | bytes 1 | tf_op jit(solution)/shard_map/grads_own_ffn_1/pallas_call | solution.py:51
  235.9 4.7 %grads_out_ffn_2.1 = bf16[1280,1920]{1,0:T(8,128)(2,1)} custom-call(bf16[256,2560]{1,0:T(8,128)(2,1)} %get-tuple-element.867.refs_0_.refs_1_, bf16[256,2560]{1,0:T(8,128)(2,1)} %cotangent.1.refs_5_.refs_1_.refs_3_.cot_ref, bf16[256,1280]{1,0:T(8,128)(2,1)} %get-tuple-element.869.refs_2_, bf16[256,640]{1,0:T(8,128)(2,1)} %get-tuple-element.870.refs_3_.refs_2_), custom_call_target="tpu_custom_call" | custom-call | flops 1 | bytes 1 | tf_op jit(solution)/shard_map/grads_out_ffn_2/pallas_call | solution.py:51
  240.6 3.1 collective-permute-done.53.refs_2_.refs_1_
  250.3 2.4 collective-permute-start.55
  252.7 9.0 %ffn_out.1 = (f32[64,2560]{1,0:T(8,128)}, f32[64,2560]{1,0:T(8,128)}, bf16[128,2560]{1,0:T(8,128)(2,1)}) custom-call(s32[2]{0:T(128)} %pad_add_fusion.z_ref.refs_0_, bf16[256,640]{1,0:T(8,128)(2,1)} %get-tuple-element.819.refs_3_.refs_0_, bf16[256,640]{1,0:T(8,128)(2,1)} %get-tuple-element.820.refs_3_.refs_1_, ...), custom_call_target="tpu_custom_call" | custom-call | flops 1 | bytes 1 | tf_op jit(solution)/shard_map/ffn_out/pallas_call | solution.py:51
  261.8 4.8 %collective-permute-done.55.o2 = bf16[64,2560]{1,0:T(8,128)(2,1)S(1)} collective-permute-done((bf16[64,2560]{1,0:T(8,128)(2,1)S(1)}, bf16[64,2560]{1,0:T(8,128)(2,1)S(1)}, u32[]{:S(2)}, u32[]{:S(2)}) %collective-permute-start.55) | collective-permute-done | bytes 327712 | tf_op jit(solution)/shard_map/ppermute | solution.py:749
  267.3 3.3 second_back.1
  270.7 2.7 collective-permute-start.58
  273.3 7.2 %grads_own_ffn_2.1 = (f32[320,1920]{1,0:T(8,128)}, f32[160,1920]{1,0:T(8,128)}, f32[160,1920]{1,0:T(8,128)}, bf16[480,1920]{1,0:T(8,128)(2,1)}, bf16[480,1920]{1,0:T(8,128)(2,1)}) custom-call(bf16[256,2560]{1,0:T(8,128)(2,1)} %get-tuple-element.867.refs_0_.refs_1_, bf16[256,2560]{1,0:T(8,128)(2,1)} %cotangent.1.refs_5_.refs_1_.refs_3_.cot_ref, ...), custom_call_target="tpu_custom_call" | custom-call | flops 1 | bytes 1 | tf_op jit(solution)/shard_map/grads_own_ffn_2/pallas_call | solution.py:51
  280.5 3.1 relay_0.1
  287.3 2.2 collective-permute-start.69
  289.5 4.7 %collective-permute-done.62.p3 = bf16[64,2560]{1,0:T(8,128)(2,1)} collective-permute-done((bf16[64,2560]{1,0:T(8,128)(2,1)}, bf16[64,2560]{1,0:T(8,128)(2,1)}, u32[]{:S(2)}, u32[]{:S(2)}) %collective-permute-start.62) | collective-permute-done | bytes 327712 | tf_op jit(solution)/shard_map/ppermute | solution.py:749
  294.3 11.1 %backward_scan.1 = (bf16[256,2560]{1,0:T(8,128)(2,1)}, bf16[256,640]{1,0:T(8,128)(2,1)}, f32[256,640]{1,0:T(8,128)}, bf16[256,640]{1,0:T(8,128)(2,1)}, f32[256,6...) custom-call(s32[2]{0:T(128)} %pad_add_fusion.z_ref.refs_0_, ...), custom_call_target="tpu_custom_call" | custom-call | flops 1 | bytes 1 | tf_op jit(solution)/shard_map/backward_scan/pallas_call | solution.py:1173
  305.6 2.5 collective-permute-done.63.b_ref.o1
  308.3 3.9 grads_out_yo.1
  312.3 3.2 relay_1.1
  323.3 8.5 %collective-permute-done.67.r1 = bf16[256,640]{1,0:T(8,128)(2,1)S(1)} collective-permute-done((bf16[256,640]{1,0:T(8,128)(2,1)}, bf16[256,640]{1,0:T(8,128)(2,1)S(1)}, u32[]{:S(2)}, u32[]{:S(2)}) %collective-permute-start.67) | collective-permute-done | bytes 327712 | tf_op jit(solution)/shard_map/ppermute | solution.py:749
  332.5 2.3 collective-permute-start.71
  339.4 10.7 %conv_back.1 = (bf16[256,640]{1,0:T(8,128)(2,1)}, f32[8,640]{1,0:T(8,128)}, f32[1,2560]{1,0:T(1,128)}, f32[64,2560]{1,0:T(8,128)}, bf16[64,2560]{1,0:T(8,128)(2,...) custom-call(s32[2]{0:T(128)} %pad_add_fusion.z_ref.refs_0_, f32[256,640]{1,0:T(8,128)} %get-tuple-element.952.direct_ref, ...), custom_call_target="tpu_custom_call" | custom-call | flops 1 | bytes 1 | tf_op jit(solution)/shard_map/conv_back/pallas_call | solution.py:1208
  350.4 3.6 collective-permute-start.72
  354.1 2.9 grads_out_x.1
  357.0 5.9 %grads_own_yo.1 = (f32[320,1280]{1,0:T(8,128)}, f32[160,1280]{1,0:T(8,128)}, f32[160,1280]{1,0:T(8,128)}, bf16[320,1280]{1,0:T(8,128)(2,1)}, bf16[320,1280]{1,0:T(8,128)(2,1)}) custom-call(bf16[256,2560]{1,0:T(8,128)(2,1)} %get-tuple-element.1034.nf_ref.refs_0_, bf16[256,2560]{1,0:T(8,128)(2,1)} %get-tuple-element.995.refs_1_, ...), custom_call_target="tpu_custom_call" | custom-call | flops 1 | bytes 1 | tf_op jit(solution)/shard_map/grads_own_yo/pallas_call | solution.py:51
  362.9 3.2 relay_2.1
  371.5 14.1 %collective-permute-done.77.o1 = bf16[64,2560]{1,0:T(8,128)(2,1)S(1)} collective-permute-done((bf16[64,2560]{1,0:T(8,128)(2,1)S(1)}, bf16[64,2560]{1,0:T(8,128)(2,1)S(1)}, u32[]{:S(2)}, u32[]{:S(2)}) %collective-permute-start.77) | collective-permute-done | bytes 327712 | tf_op jit(solution)/shard_map/ppermute | solution.py:749
  388.2 4.1 first_back.1.refs_15_
  397.2 4.4 grads_own_x.1
  401.6 3.2 relay_3.1
  404.8 2.5 block_out.1.refs_5_
  415.9 8.6 %join_ffn.1 = (f32[320,1920]{1,0:T(8,128)}, f32[320,1920]{1,0:T(8,128)}, f32[320,1920]{1,0:T(8,128)}) custom-call(f32[320,1920]{1,0:T(8,128)} %get-tuple-element.1077.refs_0_, bf16[320,1920]{1,0:T(8,128)(2,1)} %copy-done.14, bf16[320,1920]{1,0:T(8,128)(2,1)} %copy-done.15, bf16[480,1920]{1,0:T(8,128)(2,1)} %copy-done, ...), custom_call_target="tpu_custom_call" | custom-call | flops 1 | bytes 1 | tf_op jit(solution)/shard_map/join_ffn/pallas_call | solution.py:51
  424.5 2.8 collective-permute-done.87
  438.2 3.5 join_yo.1
  442.4 2.7 collective-permute-done.93.refs_6_.refs_8_
  446.5 3.0 collective-permute-done.99.refs_14_
  450.9 6.7 %last.1 = (f32[640,320]{1,0:T(8,128)}, bf16[256,2560]{1,0:T(8,128)(2,1)}, f32[256,2560]{1,0:T(8,128)}, f32[10,64,256]{2,1,0:T(8,128)}, f32[10,64,256]{2,1,0:T(8,...) custom-call(s32[2]{0:T(128)} %pad_add_fusion.z_ref.refs_0_, ...), custom_call_target="tpu_custom_call" | custom-call | flops 1 | bytes 1 | tf_op jit(solution)/shard_map/last/pallas_call | solution.py:51
  (382 shorter events, 121.7 us)
Async XLA Ops:
  2.4 12.7 %collective-permute-start.1 = (bf16[320,640]{1,0:T(8,128)(2,1)S(1)}, bf16[320,640]{1,0:T(8,128)(2,1)S(1)}, u32[]{:S(2)}, u32[]{:S(2)}) collective-permute-start(bf16[320,640]{1,0:T(8,128)(2,1)S(1)} %copy.41), channel_id=1, source_target_pairs={{0,16},{4,20},{8,24},{12,28},{16,0},{20,4},{24,8},{28,12},{1,17},{... | collective-permute-start | bytes 1228808 | tf_op jit(solution)/shard_map/ppermute | solution.py:749
  26.7 29.5 %collective-permute-start.11 = (bf16[320,1280]{1,0:T(8,128)(2,1)S(1)}, bf16[320,1280]{1,0:T(8,128)(2,1)S(1)}, u32[]{:S(2)}, u32[]{:S(2)}) collective-permute-start(bf16[320,1280]{1,0:T(8,128)(2,1)S(1)} %pad_maximum_fusion.refs_0_.refs_10_), channel_id=1, source_target_pairs={{0,8},{4,12},{8,0},{12,4},{16,24},{20,28},{24,16},{28,20},{1,9},{5... | collective-permute-start | bytes 2457608 | tf_op jit(solution)/shard_map/ppermute | solution.py:749
  28.3 27.8 %collective-permute-start.12 = (bf16[320,1280]{1,0:T(8,128)(2,1)S(1)}, bf16[320,1280]{1,0:T(8,128)(2,1)S(1)}, u32[]{:S(2)}, u32[]{:S(2)}) collective-permute-start(bf16[320,1280]{1,0:T(8,128)(2,1)S(1)} %pad_maximum_fusion.refs_0_.refs_10_), channel_id=1, source_target_pairs={{0,16},{4,20},{8,24},{12,28},{16,0},{20,4},{24,8},{28,12},{1,17},{... | collective-permute-start | bytes 2457608 | tf_op jit(solution)/shard_map/ppermute | solution.py:749
  36.4 19.7 %collective-permute-start.13 = (bf16[320,1280]{1,0:T(8,128)(2,1)S(1)}, bf16[320,1280]{1,0:T(8,128)(2,1)S(1)}, u32[]{:S(2)}, u32[]{:S(2)}) collective-permute-start(bf16[320,1280]{1,0:T(8,128)(2,1)S(1)} %pad_maximum_fusion.refs_0_.refs_10_), channel_id=1, source_target_pairs={{0,4},{4,0},{8,12},{12,8},{16,20},{20,16},{24,28},{28,24},{1,5},{5... | collective-permute-start | bytes 2457608 | tf_op jit(solution)/shard_map/ppermute | solution.py:749
  36.5 17.2 %collective-permute-start.10 = (bf16[256,640]{1,0:T(8,128)(2,1)}, bf16[256,640]{1,0:T(8,128)(2,1)S(1)}, u32[]{:S(2)}, u32[]{:S(2)}) collective-permute-start(bf16[256,640]{1,0:T(8,128)(2,1)} %get-tuple-element.901.c0.refs_10_), channel_id=1, source_target_pairs={{0,1},{1,0},{2,3},{3,2},{4,5},{5,4},{6,7},{7,6},{8,9},{9,8},{10,11... | collective-permute-start | bytes 983048 | tf_op jit(solution)/shard_map/ppermute | solution.py:749
  38.2 18.0 %collective-permute-start.9 = (bf16[256,640]{1,0:T(8,128)(2,1)}, bf16[256,640]{1,0:T(8,128)(2,1)S(1)}, u32[]{:S(2)}, u32[]{:S(2)}) collective-permute-start(bf16[256,640]{1,0:T(8,128)(2,1)} %get-tuple-element.901.c0.refs_10_), channel_id=1, source_target_pairs={{0,2},{1,3},{2,0},{3,1},{4,6},{5,7},{6,4},{7,5},{8,10},{9,11},{10,... | collective-permute-start | bytes 983048 | tf_op jit(solution)/shard_map/ppermute | solution.py:749
  56.2 14.2 %collective-permute-start.17 = (bf16[320,1280]{1,0:T(8,128)(2,1)S(1)}, bf16[320,1280]{1,0:T(8,128)(2,1)S(1)}, u32[]{:S(2)}, u32[]{:S(2)}) collective-permute-start(bf16[320,1280]{1,0:T(8,128)(2,1)S(1)} %collective-permute-done.11.refs_1_.refs_11_), channel_id=1, source_target_pairs={{0,4},{4,0},{8,12},{12,8},{16,20},{20,16},{24,28},{28,24},{1,5},{5... | collective-permute-start | bytes 2457608 | tf_op jit(solution)/shard_map/ppermute | solution.py:749
  56.3 14.1 %collective-permute-start.18 = (bf16[320,1280]{1,0:T(8,128)(2,1)S(1)}, bf16[320,1280]{1,0:T(8,128)(2,1)}, u32[]{:S(2)}, u32[]{:S(2)}) collective-permute-start(bf16[320,1280]{1,0:T(8,128)(2,1)S(1)} %collective-permute-done.12.refs_2_.refs_12_), channel_id=1, source_target_pairs={{0,4},{4,0},{8,12},{12,8},{16,20},{20,16},{24,28},{28,24},{1,5},{5... | collective-permute-start | bytes 2457608 | tf_op jit(solution)/shard_map/ppermute | solution.py:749
  70.5 30.0 %collective-permute-start.23 = (bf16[320,1920]{1,0:T(8,128)(2,1)S(1)}, bf16[320,1920]{1,0:T(8,128)(2,1)}, u32[]{:S(2)}, u32[]{:S(2)}) collective-permute-start(bf16[320,1920]{1,0:T(8,128)(2,1)S(1)} %copy-done.4), channel_id=1, source_target_pairs={{0,8},{4,12},{8,0},{12,4},{16,24},{20,28},{24,16},{28,20},{1,9},{5... | collective-permute-start | bytes 3686408 | tf_op jit(solution)/shard_map/ppermute | solution.py:749
  72.0 30.0 %collective-permute-start.24 = (bf16[320,1920]{1,0:T(8,128)(2,1)S(1)}, bf16[320,1920]{1,0:T(8,128)(2,1)}, u32[]{:S(2)}, u32[]{:S(2)}) collective-permute-start(bf16[320,1920]{1,0:T(8,128)(2,1)S(1)} %copy-done.4), channel_id=1, source_target_pairs={{0,16},{4,20},{8,24},{12,28},{16,0},{20,4},{24,8},{28,12},{1,17},{... | collective-permute-start | bytes 3686408 | tf_op jit(solution)/shard_map/ppermute | solution.py:749
  88.8 13.2 %collective-permute-start.22 = (bf16[64,2560]{1,0:T(8,128)(2,1)}, bf16[64,2560]{1,0:T(8,128)(2,1)S(1)}, u32[]{:S(2)}, u32[]{:S(2)}) collective-permute-start(bf16[64,2560]{1,0:T(8,128)(2,1)} %get-tuple-element.673), channel_id=1, source_target_pairs={{0,1},{1,0},{2,3},{3,2},{4,5},{5,4},{6,7},{7,6},{8,9},{9,8},{10,11... | collective-permute-start | bytes 983048 | tf_op jit(solution)/shard_map/ppermute | solution.py:749
  89.3 36.9 %collective-permute-start.27 = (bf16[320,1920]{1,0:T(8,128)(2,1)S(1)}, bf16[320,1920]{1,0:T(8,128)(2,1)S(1)}, u32[]{:S(2)}, u32[]{:S(2)}) collective-permute-start(bf16[320,1920]{1,0:T(8,128)(2,1)S(1)} %copy-done.5), channel_id=1, source_target_pairs={{0,8},{4,12},{8,0},{12,4},{16,24},{20,28},{24,16},{28,20},{1,9},{5... | collective-permute-start | bytes 3686408 | tf_op jit(solution)/shard_map/ppermute | solution.py:749
  90.2 37.3 %collective-permute-start.28 = (bf16[320,1920]{1,0:T(8,128)(2,1)S(1)}, bf16[320,1920]{1,0:T(8,128)(2,1)}, u32[]{:S(2)}, u32[]{:S(2)}) collective-permute-start(bf16[320,1920]{1,0:T(8,128)(2,1)S(1)} %copy-done.5), channel_id=1, source_target_pairs={{0,16},{4,20},{8,24},{12,28},{16,0},{20,4},{24,8},{28,12},{1,17},{... | collective-permute-start | bytes 3686408 | tf_op jit(solution)/shard_map/ppermute | solution.py:749
  102.0 25.6 %collective-permute-start.29 = (bf16[320,1920]{1,0:T(8,128)(2,1)}, bf16[320,1920]{1,0:T(8,128)(2,1)S(1)}, u32[]{:S(2)}, u32[]{:S(2)}) collective-permute-start(bf16[320,1920]{1,0:T(8,128)(2,1)} %collective-permute-done.23.refs_7_.refs_4_), channel_id=1, source_target_pairs={{0,4},{4,0},{8,12},{12,8},{16,20},{20,16},{24,28},{28,24},{1,5},{5... | collective-permute-start | bytes 3686408 | tf_op jit(solution)/shard_map/ppermute | solution.py:749
  104.7 21.6 %collective-permute-start.26 = (bf16[64,2560]{1,0:T(8,128)(2,1)}, bf16[64,2560]{1,0:T(8,128)(2,1)S(1)}, u32[]{:S(2)}, u32[]{:S(2)}) collective-permute-start(bf16[64,2560]{1,0:T(8,128)(2,1)} %get-tuple-element.681), channel_id=1, source_target_pairs={{0,1},{1,0},{2,3},{3,2},{4,5},{5,4},{6,7},{7,6},{8,9},{9,8},{10,11... | collective-permute-start | bytes 983048 | tf_op jit(solution)/shard_map/ppermute | solution.py:749
  105.1 21.1 %collective-permute-start.25 = (bf16[64,2560]{1,0:T(8,128)(2,1)}, bf16[64,2560]{1,0:T(8,128)(2,1)S(1)}, u32[]{:S(2)}, u32[]{:S(2)}) collective-permute-start(bf16[64,2560]{1,0:T(8,128)(2,1)} %first_add.1), channel_id=1, source_target_pairs={{0,2},{1,3},{2,0},{3,1},{4,6},{5,7},{6,4},{7,5},{8,10},{9,11},{10,... | collective-permute-start | bytes 983048 | tf_op jit(solution)/shard_map/ppermute | solution.py:749
  128.1 29.7 %collective-permute-start.36 = (bf16[320,1920]{1,0:T(8,128)(2,1)}, bf16[320,1920]{1,0:T(8,128)(2,1)}, u32[]{:S(2)}, u32[]{:S(2)}) collective-permute-start(bf16[320,1920]{1,0:T(8,128)(2,1)} %collective-permute-done.24.refs_8_.refs_5_), channel_id=1, source_target_pairs={{0,8},{4,12},{8,0},{12,4},{16,24},{20,28},{24,16},{28,20},{1,9},{5... | collective-permute-start | bytes 3686408 | tf_op jit(solution)/shard_map/ppermute | solution.py:749
  128.7 29.2 %collective-permute-start.37 = (bf16[320,1920]{1,0:T(8,128)(2,1)S(1)}, bf16[320,1920]{1,0:T(8,128)(2,1)}, u32[]{:S(2)}, u32[]{:S(2)}) collective-permute-start(bf16[320,1920]{1,0:T(8,128)(2,1)S(1)} %collective-permute-done.27.refs_15_.refs_12_), channel_id=1, source_target_pairs={{0,16},{4,20},{8,24},{12,28},{16,0},{20,4},{24,8},{28,12},{1,17},{... | collective-permute-start | bytes 3686408 | tf_op jit(solution)/shard_map/ppermute | solution.py:749
  134.3 16.7 %collective-permute-start.34 = (bf16[64,2560]{1,0:T(8,128)(2,1)}, bf16[64,2560]{1,0:T(8,128)(2,1)S(1)}, u32[]{:S(2)}, u32[]{:S(2)}) collective-permute-start(bf16[64,2560]{1,0:T(8,128)(2,1)} %get-tuple-element.717.refs_1_), channel_id=1, source_target_pairs={{0,1},{1,0},{2,3},{3,2},{4,5},{5,4},{6,7},{7,6},{8,9},{9,8},{10,11... | collective-permute-start | bytes 983048 | tf_op jit(solution)/shard_map/ppermute | solution.py:749
  134.8 17.7 %collective-permute-start.33 = (bf16[64,2560]{1,0:T(8,128)(2,1)}, bf16[64,2560]{1,0:T(8,128)(2,1)S(1)}, u32[]{:S(2)}, u32[]{:S(2)}) collective-permute-start(bf16[64,2560]{1,0:T(8,128)(2,1)} %get-tuple-element.717.refs_1_), channel_id=1, source_target_pairs={{0,2},{1,3},{2,0},{3,1},{4,6},{5,7},{6,4},{7,5},{8,10},{9,11},{10,... | collective-permute-start | bytes 983048 | tf_op jit(solution)/shard_map/ppermute | solution.py:749
  160.9 30.3 %collective-permute-start.42 = (bf16[320,1920]{1,0:T(8,128)(2,1)}, bf16[320,1920]{1,0:T(8,128)(2,1)S(1)}, u32[]{:S(2)}, u32[]{:S(2)}) collective-permute-start(bf16[320,1920]{1,0:T(8,128)(2,1)} %shard.5.refs_4_.refs_19_), channel_id=1, source_target_pairs={{0,8},{4,12},{8,0},{12,4},{16,24},{20,28},{24,16},{28,20},{1,9},{5... | collective-permute-start | bytes 3686408 | tf_op jit(solution)/shard_map/ppermute | solution.py:749
  161.4 29.8 %collective-permute-start.43 = (bf16[320,1920]{1,0:T(8,128)(2,1)}, bf16[320,1920]{1,0:T(8,128)(2,1)S(1)}, u32[]{:S(2)}, u32[]{:S(2)}) collective-permute-start(bf16[320,1920]{1,0:T(8,128)(2,1)} %shard.5.refs_4_.refs_19_), channel_id=1, source_target_pairs={{0,16},{4,20},{8,24},{12,28},{16,0},{20,4},{24,8},{28,12},{1,17},{... | collective-permute-start | bytes 3686408 | tf_op jit(solution)/shard_map/ppermute | solution.py:749
  167.9 23.3 %collective-permute-start.41 = (bf16[320,1920]{1,0:T(8,128)(2,1)}, bf16[320,1920]{1,0:T(8,128)(2,1)S(1)}, u32[]{:S(2)}, u32[]{:S(2)}) collective-permute-start(bf16[320,1920]{1,0:T(8,128)(2,1)} %shard.5.refs_4_.refs_19_), channel_id=1, source_target_pairs={{0,4},{4,0},{8,12},{12,8},{16,20},{20,16},{24,28},{28,24},{1,5},{5... | collective-permute-start | bytes 3686408 | tf_op jit(solution)/shard_map/ppermute | solution.py:749
  191.2 12.1 %collective-permute-start.48 = (bf16[1280,1920]{1,0:T(8,128)(2,1)}, bf16[1280,1920]{1,0:T(8,128)(2,1)}, u32[]{:S(2)}, u32[]{:S(2)}) collective-permute-start(bf16[1280,1920]{1,0:T(8,128)(2,1)} %grads_out_ffn_0.1), channel_id=1, source_target_pairs={{0,4},{4,0},{8,12},{12,8},{16,20},{20,16},{24,28},{28,24},{1,5},{5... | collective-permute-start | bytes 14745608 | tf_op jit(solution)/shard_map/ppermute | solution.py:749
  194.1 16.4 %collective-permute-start.45 = (bf16[160,1920]{1,0:T(8,128)(2,1)}, bf16[160,1920]{1,0:T(8,128)(2,1)}, u32[]{:S(2)}, u32[]{:S(2)}) collective-permute-start(bf16[160,1920]{1,0:T(8,128)(2,1)} %slice.35), channel_id=1, source_target_pairs={{0,8},{4,12},{8,0},{12,4},{16,24},{20,28},{24,16},{28,20},{1,9},{5... | collective-permute-start | bytes 1843208 | tf_op jit(solution)/shard_map/ppermute | solution.py:749
  194.8 16.1 %collective-permute-start.44 = (bf16[160,1920]{1,0:T(8,128)(2,1)}, bf16[160,1920]{1,0:T(8,128)(2,1)}, u32[]{:S(2)}, u32[]{:S(2)}) collective-permute-start(bf16[160,1920]{1,0:T(8,128)(2,1)} %slice.34), channel_id=1, source_target_pairs={{0,16},{4,20},{8,24},{12,28},{16,0},{20,4},{24,8},{28,12},{1,17},{... | collective-permute-start | bytes 1843208 | tf_op jit(solution)/shard_map/ppermute | solution.py:749
  214.1 13.1 %collective-permute-start.51 = (bf16[1280,1920]{1,0:T(8,128)(2,1)}, bf16[1280,1920]{1,0:T(8,128)(2,1)}, u32[]{:S(2)}, u32[]{:S(2)}) collective-permute-start(bf16[1280,1920]{1,0:T(8,128)(2,1)} %grads_out_ffn_1.1), channel_id=1, source_target_pairs={{0,4},{4,0},{8,12},{12,8},{16,20},{20,16},{24,28},{28,24},{1,5},{5... | collective-permute-start | bytes 14745608 | tf_op jit(solution)/shard_map/ppermute | solution.py:749
  214.2 29.5 %collective-permute-start.53 = (bf16[320,1920]{1,0:T(8,128)(2,1)}, bf16[320,1920]{1,0:T(8,128)(2,1)S(1)}, u32[]{:S(2)}, u32[]{:S(2)}) collective-permute-start(bf16[320,1920]{1,0:T(8,128)(2,1)} %get-tuple-element.799), channel_id=1, source_target_pairs={{0,8},{4,12},{8,0},{12,4},{16,24},{20,28},{24,16},{28,20},{1,9},{5... | collective-permute-start | bytes 3686408 | tf_op jit(solution)/shard_map/ppermute | solution.py:749
  215.5 29.2 %collective-permute-start.54 = (bf16[320,1920]{1,0:T(8,128)(2,1)}, bf16[320,1920]{1,0:T(8,128)(2,1)S(1)}, u32[]{:S(2)}, u32[]{:S(2)}) collective-permute-start(bf16[320,1920]{1,0:T(8,128)(2,1)} %get-tuple-element.800), channel_id=1, source_target_pairs={{0,16},{4,20},{8,24},{12,28},{16,0},{20,4},{24,8},{28,12},{1,17},{... | collective-permute-start | bytes 3686408 | tf_op jit(solution)/shard_map/ppermute | solution.py:749
  227.2 17.6 %collective-permute-start.52 = (bf16[64,2560]{1,0:T(8,128)(2,1)}, bf16[64,2560]{1,0:T(8,128)(2,1)S(1)}, u32[]{:S(2)}, u32[]{:S(2)}) collective-permute-start(bf16[64,2560]{1,0:T(8,128)(2,1)} %get-tuple-element.796), channel_id=1, source_target_pairs={{0,1},{1,0},{2,3},{3,2},{4,5},{5,4},{6,7},{7,6},{8,9},{9,8},{10,11... | collective-permute-start | bytes 983048 | tf_op jit(solution)/shard_map/ppermute | solution.py:749
  244.8 21.9 %collective-permute-start.57 = (bf16[1280,1920]{1,0:T(8,128)(2,1)}, bf16[1280,1920]{1,0:T(8,128)(2,1)}, u32[]{:S(2)}, u32[]{:S(2)}) collective-permute-start(bf16[1280,1920]{1,0:T(8,128)(2,1)} %grads_out_ffn_2.1), channel_id=1, source_target_pairs={{0,4},{4,0},{8,12},{12,8},{16,20},{20,16},{24,28},{28,24},{1,5},{5... | collective-permute-start | bytes 14745608 | tf_op jit(solution)/shard_map/ppermute | solution.py:749
  245.9 15.9 %collective-permute-start.56 = (bf16[64,2560]{1,0:T(8,128)(2,1)}, bf16[64,2560]{1,0:T(8,128)(2,1)S(1)}, u32[]{:S(2)}, u32[]{:S(2)}) collective-permute-start(bf16[64,2560]{1,0:T(8,128)(2,1)} %get-tuple-element.816), channel_id=1, source_target_pairs={{0,1},{1,0},{2,3},{3,2},{4,5},{5,4},{6,7},{7,6},{8,9},{9,8},{10,11... | collective-permute-start | bytes 983048 | tf_op jit(solution)/shard_map/ppermute | solution.py:749
  247.6 36.0 %collective-permute-start.60 = (bf16[320,1920]{1,0:T(8,128)(2,1)}, bf16[320,1920]{1,0:T(8,128)(2,1)S(1)}, u32[]{:S(2)}, u32[]{:S(2)}) collective-permute-start(bf16[320,1920]{1,0:T(8,128)(2,1)} %get-tuple-element.859), channel_id=1, source_target_pairs={{0,8},{4,12},{8,0},{12,4},{16,24},{20,28},{24,16},{28,20},{1,9},{5... | collective-permute-start | bytes 3686408 | tf_op jit(solution)/shard_map/ppermute | solution.py:749
  248.3 35.3 %collective-permute-start.61 = (bf16[320,1920]{1,0:T(8,128)(2,1)}, bf16[320,1920]{1,0:T(8,128)(2,1)S(1)}, u32[]{:S(2)}, u32[]{:S(2)}) collective-permute-start(bf16[320,1920]{1,0:T(8,128)(2,1)} %get-tuple-element.860), channel_id=1, source_target_pairs={{0,16},{4,20},{8,24},{12,28},{16,0},{20,4},{24,8},{28,12},{1,17},{... | collective-permute-start | bytes 3686408 | tf_op jit(solution)/shard_map/ppermute | solution.py:749
  250.3 16.3 %collective-permute-start.55 = (bf16[64,2560]{1,0:T(8,128)(2,1)S(1)}, bf16[64,2560]{1,0:T(8,128)(2,1)S(1)}, u32[]{:S(2)}, u32[]{:S(2)}) collective-permute-start(bf16[64,2560]{1,0:T(8,128)(2,1)S(1)} %add_convert_fusion.2), channel_id=1, source_target_pairs={{0,2},{1,3},{2,0},{3,1},{4,6},{5,7},{6,4},{7,5},{8,10},{9,11},{10,... | collective-permute-start | bytes 983048 | tf_op jit(solution)/shard_map/ppermute | solution.py:749
  270.7 14.2 %collective-permute-start.59 = (bf16[64,2560]{1,0:T(8,128)(2,1)}, bf16[64,2560]{1,0:T(8,128)(2,1)S(1)}, u32[]{:S(2)}, u32[]{:S(2)}) collective-permute-start(bf16[64,2560]{1,0:T(8,128)(2,1)} %get-tuple-element.887.p0), channel_id=1, source_target_pairs={{0,1},{1,0},{2,3},{3,2},{4,5},{5,4},{6,7},{7,6},{8,9},{9,8},{10,11... | collective-permute-start | bytes 983048 | tf_op jit(solution)/shard_map/ppermute | solution.py:749
  270.7 15.6 %collective-permute-start.58 = (bf16[64,2560]{1,0:T(8,128)(2,1)}, bf16[64,2560]{1,0:T(8,128)(2,1)}, u32[]{:S(2)}, u32[]{:S(2)}) collective-permute-start(bf16[64,2560]{1,0:T(8,128)(2,1)} %get-tuple-element.887.p0), channel_id=1, source_target_pairs={{0,2},{1,3},{2,0},{3,1},{4,6},{5,7},{6,4},{7,5},{8,10},{9,11},{10,... | collective-permute-start | bytes 983048 | tf_op jit(solution)/shard_map/ppermute | solution.py:749
  286.5 45.3 %collective-permute-start.68 = (bf16[480,1920]{1,0:T(8,128)(2,1)}, bf16[480,1920]{1,0:T(8,128)(2,1)S(1)}, u32[]{:S(2)}, u32[]{:S(2)}) collective-permute-start(bf16[480,1920]{1,0:T(8,128)(2,1)} %get-tuple-element.940), channel_id=1, source_target_pairs={{0,8},{4,12},{8,0},{12,4},{16,24},{20,28},{24,16},{28,20},{1,9},{5... | collective-permute-start | bytes 5529608 | tf_op jit(solution)/shard_map/ppermute | solution.py:749
  287.3 44.5 %collective-permute-start.69 = (bf16[480,1920]{1,0:T(8,128)(2,1)}, bf16[480,1920]{1,0:T(8,128)(2,1)}, u32[]{:S(2)}, u32[]{:S(2)}) collective-permute-start(bf16[480,1920]{1,0:T(8,128)(2,1)} %get-tuple-element.941), channel_id=1, source_target_pairs={{0,16},{4,20},{8,24},{12,28},{16,0},{20,4},{24,8},{28,12},{1,17},{... | collective-permute-start | bytes 5529608 | tf_op jit(solution)/shard_map/ppermute | solution.py:749
  294.2 13.9 %collective-permute-start.63 = (bf16[128,2560]{1,0:T(8,128)(2,1)}, bf16[128,2560]{1,0:T(8,128)(2,1)}, u32[]{:S(2)}, u32[]{:S(2)}) collective-permute-start(bf16[128,2560]{1,0:T(8,128)(2,1)} %get-tuple-element.912), channel_id=1, source_target_pairs={{0,1},{1,0},{2,3},{3,2},{4,5},{5,4},{6,7},{7,6},{8,9},{9,8},{10,11... | collective-permute-start | bytes 1966088 | tf_op jit(solution)/shard_map/ppermute | solution.py:749
  316.1 15.7 %collective-permute-start.67 = (bf16[256,640]{1,0:T(8,128)(2,1)}, bf16[256,640]{1,0:T(8,128)(2,1)S(1)}, u32[]{:S(2)}, u32[]{:S(2)}) collective-permute-start(bf16[256,640]{1,0:T(8,128)(2,1)} %get-tuple-element.939), channel_id=1, source_target_pairs={{0,1},{1,0},{2,3},{3,2},{4,5},{5,4},{6,7},{7,6},{8,9},{9,8},{10,11... | collective-permute-start | bytes 983048 | tf_op jit(solution)/shard_map/ppermute | solution.py:749
  317.9 13.9 %collective-permute-start.66 = (bf16[256,640]{1,0:T(8,128)(2,1)S(1)}, bf16[256,640]{1,0:T(8,128)(2,1)}, u32[]{:S(2)}, u32[]{:S(2)}) collective-permute-start(bf16[256,640]{1,0:T(8,128)(2,1)S(1)} %add_convert_fusion.1), channel_id=1, source_target_pairs={{0,2},{1,3},{2,0},{3,1},{4,6},{5,7},{6,4},{7,5},{8,10},{9,11},{10,... | collective-permute-start | bytes 983048 | tf_op jit(solution)/shard_map/ppermute | solution.py:749
  331.8 18.6 %collective-permute-start.70 = (bf16[1280,1280]{1,0:T(8,128)(2,1)}, bf16[1280,1280]{1,0:T(8,128)(2,1)}, u32[]{:S(2)}, u32[]{:S(2)}) collective-permute-start(bf16[1280,1280]{1,0:T(8,128)(2,1)} %grads_out_yo.1), channel_id=1, source_target_pairs={{0,4},{4,0},{8,12},{12,8},{16,20},{20,16},{24,28},{28,24},{1,5},{5... | collective-permute-start | bytes 9830408 | tf_op jit(solution)/shard_map/ppermute | solution.py:749
  332.5 17.9 %collective-permute-start.71 = (bf16[64,2560]{1,0:T(8,128)(2,1)}, bf16[64,2560]{1,0:T(8,128)(2,1)}, u32[]{:S(2)}, u32[]{:S(2)}) collective-permute-start(bf16[64,2560]{1,0:T(8,128)(2,1)} %out_add.1), channel_id=1, source_target_pairs={{0,2},{1,3},{2,0},{3,1},{4,6},{5,7},{6,4},{7,5},{8,10},{9,11},{10,... | collective-permute-start | bytes 983048 | tf_op jit(solution)/shard_map/ppermute | solution.py:749
  334.8 31.3 %collective-permute-start.73 = (bf16[160,1920]{1,0:T(8,128)(2,1)}, bf16[160,1920]{1,0:T(8,128)(2,1)S(1)}, u32[]{:S(2)}, u32[]{:S(2)}) collective-permute-start(bf16[160,1920]{1,0:T(8,128)(2,1)} %get-tuple-element.1003), channel_id=1, source_target_pairs={{0,8},{4,12},{8,0},{12,4},{16,24},{20,28},{24,16},{28,20},{1,9},{5... | collective-permute-start | bytes 1843208 | tf_op jit(solution)/shard_map/ppermute | solution.py:749
  335.6 30.5 %collective-permute-start.74 = (bf16[160,1920]{1,0:T(8,128)(2,1)}, bf16[160,1920]{1,0:T(8,128)(2,1)}, u32[]{:S(2)}, u32[]{:S(2)}) collective-permute-start(bf16[160,1920]{1,0:T(8,128)(2,1)} %get-tuple-element.1004), channel_id=1, source_target_pairs={{0,16},{4,20},{8,24},{12,28},{16,0},{20,4},{24,8},{28,12},{1,17},{... | collective-permute-start | bytes 1843208 | tf_op jit(solution)/shard_map/ppermute | solution.py:749
  337.6 28.5 %collective-permute-start.75 = (bf16[5,4,64,128]{3,2,1,0:T(8,128)(2,1)S(1)}, bf16[5,4,64,128]{3,2,1,0:T(8,128)(2,1)}, u32[]{:S(2)}, u32[]{:S(2)}) collective-permute-start(bf16[5,4,64,128]{3,2,1,0:T(8,128)(2,1)S(1)} %copy-done.44), channel_id=1, source_target_pairs={{0,8},{4,12},{8,0},{12,4},{16,24},{20,28},{24,16},{28,20},{1,9},{5... | collective-permute-start | bytes 983048 | tf_op jit(solution)/shard_map/ppermute | solution.py:749
  350.4 15.7 %collective-permute-start.72 = (bf16[64,2560]{1,0:T(8,128)(2,1)}, bf16[64,2560]{1,0:T(8,128)(2,1)S(1)}, u32[]{:S(2)}, u32[]{:S(2)}) collective-permute-start(bf16[64,2560]{1,0:T(8,128)(2,1)} %get-tuple-element.989), channel_id=1, source_target_pairs={{0,1},{1,0},{2,3},{3,2},{4,5},{5,4},{6,7},{7,6},{8,9},{9,8},{10,11... | collective-permute-start | bytes 983048 | tf_op jit(solution)/shard_map/ppermute | solution.py:749
  366.1 22.0 %collective-permute-start.78 = (bf16[1280,640]{1,0:T(8,128)(2,1)}, bf16[1280,640]{1,0:T(8,128)(2,1)S(1)}, u32[]{:S(2)}, u32[]{:S(2)}) collective-permute-start(bf16[1280,640]{1,0:T(8,128)(2,1)} %grads_out_x.1), channel_id=1, source_target_pairs={{0,4},{4,0},{8,12},{12,8},{16,20},{20,16},{24,28},{28,24},{1,5},{5... | collective-permute-start | bytes 4915208 | tf_op jit(solution)/shard_map/ppermute | solution.py:749
  366.9 20.1 %collective-permute-start.79 = (bf16[320,1280]{1,0:T(8,128)(2,1)}, bf16[320,1280]{1,0:T(8,128)(2,1)S(1)}, u32[]{:S(2)}, u32[]{:S(2)}) collective-permute-start(bf16[320,1280]{1,0:T(8,128)(2,1)} %get-tuple-element.1021), channel_id=1, source_target_pairs={{0,8},{4,12},{8,0},{12,4},{16,24},{20,28},{24,16},{28,20},{1,9},{5... | collective-permute-start | bytes 2457608 | tf_op jit(solution)/shard_map/ppermute | solution.py:749
  368.3 19.9 %collective-permute-start.80 = (bf16[320,1280]{1,0:T(8,128)(2,1)}, bf16[320,1280]{1,0:T(8,128)(2,1)S(1)}, u32[]{:S(2)}, u32[]{:S(2)}) collective-permute-start(bf16[320,1280]{1,0:T(8,128)(2,1)} %get-tuple-element.1022), channel_id=1, source_target_pairs={{0,16},{4,20},{8,24},{12,28},{16,0},{20,4},{24,8},{28,12},{1,17},{... | collective-permute-start | bytes 2457608 | tf_op jit(solution)/shard_map/ppermute | solution.py:749
  369.4 16.2 %collective-permute-start.77 = (bf16[64,2560]{1,0:T(8,128)(2,1)S(1)}, bf16[64,2560]{1,0:T(8,128)(2,1)S(1)}, u32[]{:S(2)}, u32[]{:S(2)}) collective-permute-start(bf16[64,2560]{1,0:T(8,128)(2,1)S(1)} %copy-done.83), channel_id=1, source_target_pairs={{0,1},{1,0},{2,3},{3,2},{4,5},{5,4},{6,7},{7,6},{8,9},{9,8},{10,11... | collective-permute-start | bytes 983048 | tf_op jit(solution)/shard_map/ppermute | solution.py:749
  369.5 16.1 %collective-permute-start.76 = (bf16[64,2560]{1,0:T(8,128)(2,1)S(1)}, bf16[64,2560]{1,0:T(8,128)(2,1)S(1)}, u32[]{:S(2)}, u32[]{:S(2)}) collective-permute-start(bf16[64,2560]{1,0:T(8,128)(2,1)S(1)} %add_convert_fusion), channel_id=1, source_target_pairs={{0,2},{1,3},{2,0},{3,1},{4,6},{5,7},{6,4},{7,5},{8,10},{9,11},{10,... | collective-permute-start | bytes 983048 | tf_op jit(solution)/shard_map/ppermute | solution.py:749
  392.3 17.0 %collective-permute-start.83 = (bf16[160,1920]{1,0:T(8,128)(2,1)}, bf16[160,1920]{1,0:T(8,128)(2,1)}, u32[]{:S(2)}, u32[]{:S(2)}) collective-permute-start(bf16[160,1920]{1,0:T(8,128)(2,1)} %get-tuple-element.1040), channel_id=1, source_target_pairs={{0,8},{4,12},{8,0},{12,4},{16,24},{20,28},{24,16},{28,20},{1,9},{5... | collective-permute-start | bytes 1843208 | tf_op jit(solution)/shard_map/ppermute | solution.py:749
  393.1 16.2 %collective-permute-start.84 = (bf16[160,1920]{1,0:T(8,128)(2,1)}, bf16[160,1920]{1,0:T(8,128)(2,1)S(1)}, u32[]{:S(2)}, u32[]{:S(2)}) collective-permute-start(bf16[160,1920]{1,0:T(8,128)(2,1)} %get-tuple-element.1041), channel_id=1, source_target_pairs={{0,16},{4,20},{8,24},{12,28},{16,0},{20,4},{24,8},{28,12},{1,17},{... | collective-permute-start | bytes 1843208 | tf_op jit(solution)/shard_map/ppermute | solution.py:749
  393.7 15.5 %collective-permute-start.82 = (bf16[64,2560]{1,0:T(8,128)(2,1)}, bf16[64,2560]{1,0:T(8,128)(2,1)S(1)}, u32[]{:S(2)}, u32[]{:S(2)}) collective-permute-start(bf16[64,2560]{1,0:T(8,128)(2,1)} %first_back.1.refs_15_), channel_id=1, source_target_pairs={{0,1},{1,0},{2,3},{3,2},{4,5},{5,4},{6,7},{7,6},{8,9},{9,8},{10,11... | collective-permute-start | bytes 983048 | tf_op jit(solution)/shard_map/ppermute | solution.py:749
  393.7 15.5 %collective-permute-start.81 = (bf16[64,2560]{1,0:T(8,128)(2,1)}, bf16[64,2560]{1,0:T(8,128)(2,1)S(1)}, u32[]{:S(2)}, u32[]{:S(2)}) collective-permute-start(bf16[64,2560]{1,0:T(8,128)(2,1)} %first_back.1.refs_15_), channel_id=1, source_target_pairs={{0,2},{1,3},{2,0},{3,1},{4,6},{5,7},{6,4},{7,5},{8,10},{9,11},{10,... | collective-permute-start | bytes 983048 | tf_op jit(solution)/shard_map/ppermute | solution.py:749
  395.9 13.3 %collective-permute-start.85 = (f32[2,2560]{1,0:T(2,128)S(1)}, f32[2,2560]{1,0:T(2,128)S(1)}, u32[]{:S(2)}, u32[]{:S(2)}) collective-permute-start(f32[2,2560]{1,0:T(2,128)S(1)} %pad_maximum_fusion.2), channel_id=1, source_target_pairs={{0,1},{1,0},{2,3},{3,2},{4,5},{5,4},{6,7},{7,6},{8,9},{9,8},{10,11... | collective-permute-start | bytes 61448 | tf_op jit(solution)/shard_map/ppermute | solution.py:749
  409.3 19.1 %collective-permute-start.88 = (bf16[640,640]{1,0:T(8,128)(2,1)}, bf16[640,640]{1,0:T(8,128)(2,1)S(1)}, u32[]{:S(2)}, u32[]{:S(2)}) collective-permute-start(bf16[640,640]{1,0:T(8,128)(2,1)} %get-tuple-element.1070), channel_id=1, source_target_pairs={{0,8},{4,12},{8,0},{12,4},{16,24},{20,28},{24,16},{28,20},{1,9},{5... | collective-permute-start | bytes 2457608 | tf_op jit(solution)/shard_map/ppermute | solution.py:749
  410.6 19.0 %collective-permute-start.89 = (bf16[640,640]{1,0:T(8,128)(2,1)}, bf16[640,640]{1,0:T(8,128)(2,1)S(1)}, u32[]{:S(2)}, u32[]{:S(2)}) collective-permute-start(bf16[640,640]{1,0:T(8,128)(2,1)} %get-tuple-element.1071), channel_id=1, source_target_pairs={{0,16},{4,20},{8,24},{12,28},{16,0},{20,4},{24,8},{28,12},{1,17},{... | collective-permute-start | bytes 2457608 | tf_op jit(solution)/shard_map/ppermute | solution.py:749
  412.4 14.9 %collective-permute-start.90 = (bf16[64,2560]{1,0:T(8,128)(2,1)}, bf16[64,2560]{1,0:T(8,128)(2,1)S(1)}, u32[]{:S(2)}, u32[]{:S(2)}) collective-permute-start(bf16[64,2560]{1,0:T(8,128)(2,1)} %block_out.1.refs_5_), channel_id=1, source_target_pairs={{0,2},{1,3},{2,0},{3,1},{4,6},{5,7},{6,4},{7,5},{8,10},{9,11},{10,... | collective-permute-start | bytes 983048 | tf_op jit(solution)/shard_map/ppermute | solution.py:749
  413.6 13.7 %collective-permute-start.86 = (bf16[64,2560]{1,0:T(8,128)(2,1)S(1)}, bf16[64,2560]{1,0:T(8,128)(2,1)}, u32[]{:S(2)}, u32[]{:S(2)}) collective-permute-start(bf16[64,2560]{1,0:T(8,128)(2,1)S(1)} %collective-permute-done.81.refs_17_), channel_id=1, source_target_pairs={{0,1},{1,0},{2,3},{3,2},{4,5},{5,4},{6,7},{7,6},{8,9},{9,8},{10,11... | collective-permute-start | bytes 983048 | tf_op jit(solution)/shard_map/ppermute | solution.py:749
  414.6 12.7 %collective-permute-start.87 = (f32[2,2560]{1,0:T(2,128)S(1)}, f32[2,2560]{1,0:T(2,128)S(1)}, u32[]{:S(2)}, u32[]{:S(2)}) collective-permute-start(f32[2,2560]{1,0:T(2,128)S(1)} %add.28), channel_id=1, source_target_pairs={{0,2},{1,3},{2,0},{3,1},{4,6},{5,7},{6,4},{7,5},{8,10},{9,11},{10,... | collective-permute-start | bytes 61448 | tf_op jit(solution)/shard_map/ppermute | solution.py:749
  430.6 14.5 %collective-permute-start.93 = (bf16[128,2560]{1,0:T(8,128)(2,1)}, bf16[128,2560]{1,0:T(8,128)(2,1)S(1)}, u32[]{:S(2)}, u32[]{:S(2)}) collective-permute-start(bf16[128,2560]{1,0:T(8,128)(2,1)} %pad_maximum_fusion.1), channel_id=1, source_target_pairs={{0,1},{1,0},{2,3},{3,2},{4,5},{5,4},{6,7},{7,6},{8,9},{9,8},{10,11... | collective-permute-start | bytes 1966088 | tf_op jit(solution)/shard_map/ppermute | solution.py:749
  (120 other events, 789.2 us)
